TPU v7x, 512 devices: a whole 4x8x8 slice. The times are simulated.
512 devices in a mesh: dp: 32 (over z, x), mp: 16 (over y, core).
Axes of the slice: x: 4, y: 8, z: 8, core: 2. Of those that a mesh axis runs over, the one named last changes fastest.
Arguments:
- gradients: bfloat16 [32, 240, 28672], P('dp', None, 'mp'), may hold values from -6 to 6
- errors: float32 [32, 240, 28672], P('dp', None, 'mp'), may hold values from -4 to 4
- q_start: float32 [1, 240, 64], replicated, may hold values from -0.3 to 2.3
Outputs:
- update_grad: bfloat16 [240, 28672], P(None, 'mp')
- new_errors: float32 [32, 240, 28672], P('dp', None, 'mp')
- q_next: float32 [1, 240, 64], replicated
All inputs are finite; a program needn't handle non-finite values.
Results may differ from a plain program's by a relative error of at most 0.001.
Values sent between devices are 32-bit elements; how exact they have to be, the bound alone decides.
A program may use at most 64 MiB of HBM per device.

v0:
```python
import jax
import jax.numpy as jnp
from jax import lax
from jax.sharding import PartitionSpec as P


def orthonormal_rows(left_rows, gram_sum):
    lower = jnp.linalg.cholesky(gram_sum)
    return lax.linalg.triangular_solve(lower, left_rows, left_side=True, lower=True)


def power_round(blocks, q_old):
    highest = lax.Precision.HIGHEST
    replicas = lax.axis_size("dp")
    local_p = jnp.einsum("kdf,kdr->krf", blocks, q_old, precision=highest)
    p_mean = lax.psum(local_p, "dp") / replicas
    gram_local = jnp.einsum("krf,ksf->krs", p_mean, p_mean, precision=highest)
    gram_sum = lax.psum(gram_local, "mp")
    ortho = orthonormal_rows(p_mean, gram_sum)
    q_local = jnp.einsum("kdf,krf->kdr", blocks, ortho, precision=highest)
    q_total = lax.psum(q_local, ("dp", "mp"))
    q_next = q_total / replicas
    update = jnp.einsum("krf,kdr->kdf", ortho, q_next, precision=highest)
    return (update, blocks - update, q_next)


def on_device(gradients, errors, q_start):
    ff_rows = gradients.shape[2]
    matrix_count = q_start.shape[0]
    columns = q_start.shape[1]
    merged = gradients[0].astype(jnp.float32) + errors[0]
    blocks = merged.reshape(matrix_count, columns, ff_rows)
    update, remains, q_next = power_round(blocks, q_start)
    update_grad = update.reshape(matrix_count * columns, ff_rows).astype(jnp.bfloat16)
    return (update_grad, remains, q_next)


def solution(mesh):
    return jax.shard_map(
        on_device,
        mesh=mesh,
        in_specs=(P("dp", None, "mp"), P("dp", None, "mp"), P()),
        out_specs=(P(None, "mp"), P("dp", None, "mp"), P()),
        check_vma=False,
    )
```

profile of v0, /device:TPU:1, one launch (start us, length us, event | category | flops | bytes accessed | tf_op | source)
XLA Modules:
  0.0 344.4 jit_solution(1965901185529715759)
XLA Ops:
  7.2 0.0 copy-start
  7.2 0.0 all-reduce.2.cloned.1.call-start
  7.2 0.8 copy-done
  8.0 0.0 copy-start.2
  8.0 3.8 %convolution_bitcast_fusion = f32[1,64,1792]{2,1,0:T(8,128)} fusion(f32[1,240,1792]{2,1,0:T(8,128)} %param.4, bf16[1,240,1792]{2,1,0:T(8,128)(2,1)} %param.3, f32[1,240,64]{1,2,0:T(8,128)S(1)} %copy-done), kind=kOutput, calls=%fused_computation | convolution fusion | flops 331161600 | bytes 3100672 | tf_op jit(solution)/shard_map/kdf,kdr->krf/dot_general | solution.py:15
  11.9 0.0 copy-start.1
  11.9 0.0 all-reduce.2.cloned.1.call-update
  11.9 159.9 %all-reduce.2.cloned.1.call-done = f32[1,64,1792]{2,1,0:T(8,128)} async-done(((f32[1,64,1792]{2,1,0:T(8,128)}), f32[1,64,1792]{2,1,0:T(8,128)}) %all-reduce.2.cloned.1.call-update) | async-done | bytes 458768 | tf_op jit(solution)/shard_map/psum | solution.py:16
  171.7 1.7 convolution_bitcast_fusion.1
  173.4 47.4 %psum.22 = f32[1,64,64]{1,2,0:T(8,128)S(1)} all-reduce(f32[1,64,64]{1,2,0:T(8,128)S(1)} %convolution_bitcast_fusion.1), channel_id=1, replica_groups=mesh['dp'=32,'mp'=16] {'mp'}, use_global_device_ids=true, to_apply=%region_1.0 | all-reduce | flops 4096 | bytes 32768 | tf_op jit(solution)/shard_map/psum | solution.py:18
  220.8 0.1 copy.7
  220.9 5.8 %custom-call.7 = f32[1,64,64]{2,1,0:T(8,128)S(1)} custom-call(f32[1,64,64]{2,1,0:T(8,128)S(1)} %fusion.19), custom_call_target="Cholesky" | custom-call | tf_op jit(solution)/shard_map/jit(cholesky)/cholesky | solution.py:8
  226.8 0.6 compare_reduce_fusion
  227.4 0.7 fusion.17
  228.1 4.9 %custom-call.8 = f32[1,1,64,64]{2,3,1,0:T(8,128)S(1)} custom-call(f32[1,1,64,64]{3,2,1,0:T(8,128)S(1)} %fusion.17), custom_call_target="InvertDiagBlocksLowerTriangular" | custom-call | tf_op jit(solution)/shard_map/triangular_solve | solution.py:9
  233.0 1.6 fusion.7
  234.6 0.0 copy-done.2
  234.6 0.0 copy-done.1
  234.6 1.7 fusion.4
  236.4 98.1 %psum.23 = f32[1,240,64]{1,2,0:T(8,128)S(1)} all-reduce(f32[1,240,64]{1,2,0:T(8,128)S(1)} %fusion.4), channel_id=1, replica_groups=mesh['dp'=32,'mp'=16] {'dp','mp'}, use_global_device_ids=true, to_apply=%region_4.5 | all-reduce | flops 15360 | bytes 122880 | tf_op jit(solution)/shard_map/psum | solution.py:21
  334.5 0.0 copy-start.3
  334.5 3.1 fusion.3
  337.6 0.0 copy-done.3
  (3 shorter events, 0.0 us)
Async XLA Ops:
  7.2 0.8 copy-start
  7.2 164.6 %all-reduce.2.cloned.1.call-start = ((), (), s32[]{:S(2)}) async-start(), calls=%async_computation | async-start | bytes 917504 | tf_op jit(solution)/shard_map/psum | solution.py:16
  8.0 226.6 %copy-start.2 = (bf16[1,240,1792]{2,1,0:T(8,128)(2,1)S(1)}, bf16[1,240,1792]{2,1,0:T(8,128)(2,1)}, u32[]{:S(2)}) copy-start(bf16[1,240,1792]{2,1,0:T(8,128)(2,1)} %param.3) | copy-start | bytes 2580484
  11.9 222.8 %copy-start.1 = (f32[1,240,1792]{2,1,0:T(8,128)S(1)}, f32[1,240,1792]{2,1,0:T(8,128)}, u32[]{:S(2)}) copy-start(f32[1,240,1792]{2,1,0:T(8,128)} %param.4) | copy-start | bytes 5160964
  334.5 3.1 copy-start.3
Sparse Core Ops, SparseCore 0:
  12.0 159.6 all-reduce.1
where the time goes:
time: 345 us; the launch traced here: 344 us
  waiting for transfers between devices  160 us (46%)
  blocking collectives  145 us (42%)
  between operations  14.1 us (4%)
  other arithmetic  12.1 us (4%)
  matrix products  12 us (3%)
    psum x1, waiting for transfers between devices, power_round(): p_mean = lax.psum(local_p, 'dp') / replicas  160 us
    psum x1, blocking collectives, power_round(): q_total = lax.psum(q_local, ('dp', 'mp'))  98.1 us
    psum x1, blocking collectives, power_round(): gram_sum = lax.psum(gram_local, 'mp')  47.4 us
  transfers between devices with their start and end apart: 1, of which 1 were waited for; matrix products, arithmetic and copies ran while one was open for 0% of the time, Pallas kernels for 0%

commit v1 on v0

v1 whole, which is shorter than its diff:
```python
import jax
import jax.numpy as jnp
from jax import lax
from jax.experimental import pallas as pl
from jax.experimental.pallas import tpu as pltpu
from jax.sharding import PartitionSpec as P

MESH = pl.DeviceIdType.MESH
NX, NZ, NMP = 4, 8, 16
NDP = NX * NZ
COLS, RANK, FL = 240, 64, 1792
CHUNK = 256
NCHUNK = FL // CHUNK
HALF = FL // 2
ROWS_T = 384
F32, BF16 = jnp.float32, jnp.bfloat16
FAR_FIRST = (4, 3, 5, 2, 6, 1, 7, 0)
NEAR_FIRST = (1, 7, 2, 6, 3, 5, 4)


def split(value):
    high = value.astype(BF16)
    return high, (value - high.astype(F32)).astype(BF16)


def dot(a, b, dims):
    return lax.dot_general(a, b, (dims, ((), ())), preferred_element_type=F32)


def remote(src, dst, send, recv, target):
    return pltpu.make_async_remote_copy(
        src_ref=src, dst_ref=dst, send_sem=send, recv_sem=recv,
        device_id=target, device_id_type=MESH,
    )


def inverse_factor(gram):
    row_at = lax.broadcasted_iota(jnp.int32, (RANK, 2 * RANK), 0)
    col_at = lax.broadcasted_iota(jnp.int32, (RANK, 2 * RANK), 1)
    work = jnp.where(col_at == row_at + RANK, 1.0, gram)
    done = []
    for j in range(RANK):
        base = 8 * (j // 8)
        local = j - base
        pivot = work[local:local + 1, j:j + 1]
        row = work[local:local + 1, :]
        below = lax.broadcasted_iota(jnp.int32, work.shape, 0) > local
        factor = work[:, j:j + 1] / pivot
        work = work - jnp.where(below, factor * row, 0.0)
        if local == 7:
            done.append(work[:8])
            work = work[8:]
    full = jnp.concatenate(done, axis=0)
    diagonal = jnp.sum(jnp.where(col_at == row_at, full, 0.0), axis=1, keepdims=True)
    return (full / jnp.sqrt(diagonal))[:, RANK:]


def round_kernel(g_hbm, e_hbm, q_ref, p_out, v_out, q_out,
                 g_buf, e_buf, mh, ml, local_p, x_recv, z_send, z_recv, gathered, p_full,
                 t_send, t_recv, t_part, t_all, t_gather, g_gather, t_full, g_full,
                 load_sem, x_ssem, x_rsem, z_ssem, z_rsem, az_ssem, az_rsem, ax_ssem, ax_rsem,
                 ts_sem, tr_sem, ta_ssem, ta_rsem, tg_ssem, tg_rsem, gg_ssem, gg_rsem):
    dp = lax.axis_index("dp")
    mp = lax.axis_index("mp")
    z, x = dp // NX, dp % NX

    def load(c):
        cols = pl.ds(c * CHUNK, CHUNK)
        return (
            pltpu.make_async_copy(g_hbm.at[0, :, cols], g_buf.at[:, cols], load_sem.at[c, 0]),
            pltpu.make_async_copy(e_hbm.at[0, :, cols], e_buf.at[:, cols], load_sem.at[c, 1]),
        )

    for c in range(NCHUNK):
        for copy in load(c):
            copy.start()

    barrier = pltpu.get_barrier_semaphore()

    def greet_dp(k, carry):
        pl.semaphore_signal(barrier, inc=1, device_id=((dp + k) % NDP, mp), device_id_type=MESH)
        return carry

    def greet_mp(k, carry):
        pl.semaphore_signal(barrier, inc=1, device_id=(dp, (mp + k) % NMP), device_id_type=MESH)
        return carry

    lax.fori_loop(1, NDP, greet_dp, 0)
    lax.fori_loop(1, NMP, greet_mp, 0)

    q_high, q_low = split(q_ref[0].T)
    q_both = jnp.concatenate([q_high, q_low], axis=0)
    mh[COLS:256, :] = jnp.zeros((256 - COLS, FL), BF16)
    ml[COLS:256, :] = jnp.zeros((256 - COLS, FL), BF16)
    mh[256 + RANK:, :] = jnp.zeros((ROWS_T - 256 - RANK, FL), BF16)
    ml[256 + RANK:, :] = jnp.zeros((ROWS_T - 256 - RANK, FL), BF16)

    for c in range(NCHUNK):
        for copy in load(c):
            copy.wait()
        cols = slice(c * CHUNK, (c + 1) * CHUNK)
        merged = g_buf[:, cols].astype(F32) + e_buf[:, cols]
        high, low = split(merged)
        mh[:COLS, cols] = high
        ml[:COLS, cols] = low
        both = dot(q_both, high, ((1,), (0,)))
        part = both[:RANK] + both[RANK:] + dot(q_high, low, ((1,), (0,)))
        for xl in range(2):
            tile = part[:, xl * 128:(xl + 1) * 128]
            for xh in range(2):
                for t in range(NZ):
                    first = xh * 32 + t * 4
                    local_p[t, 2 * xh + xl, :, c * 128:(c + 1) * 128] = tile[first:first + 4]

    pl.semaphore_wait(barrier, NDP - 1 + NMP - 1)

    for k in FAR_FIRST:
        t = (z + k) % NZ
        for i in range(1, NX):
            to = (x + i) % NX
            remote(local_p.at[t, to], x_recv.at[t, i - 1], x_ssem, x_rsem.at[t], (z * NX + to, mp)).start()
    for k in FAR_FIRST:
        t = (z + k) % NZ
        remote(x_recv.at[t], x_recv.at[t], x_ssem, x_rsem.at[t], (dp, mp)).wait_recv()
        total = local_p[t, x] + x_recv[t, 0] + x_recv[t, 1] + x_recv[t, 2]
        z_send[k] = total
        if k:
            remote(z_send.at[k], z_recv.at[k - 1], z_ssem, z_rsem, (t * NX + x, mp)).start()
    remote(z_recv, z_recv, z_ssem, z_rsem, (dp, mp)).wait_recv()
    mean = z_send[0]
    for k in range(NZ - 1):
        mean = mean + z_recv[k]
    gathered[z, x] = mean * (1.0 / NDP)

    for k in NEAR_FIRST:
        remote(gathered.at[z, x], gathered.at[z, x], az_ssem, az_rsem.at[k], ((z + k) % NZ * NX + x, mp)).start()

    def on_to_x(t):
        for i in range(1, NX):
            remote(gathered.at[t, x], gathered.at[t, x], ax_ssem, ax_rsem, (z * NX + (x + i) % NX, mp)).start()

    on_to_x(z)
    remote(x_recv, x_recv, x_ssem, x_rsem.at[0], (dp, mp)).wait_send()
    remote(z_recv, z_recv, z_ssem, z_rsem, (dp, mp)).wait_send()
    for k in NEAR_FIRST:
        t = (z + NZ - k) % NZ
        remote(gathered.at[t, x], gathered.at[t, x], az_ssem, az_rsem.at[k], (dp, mp)).wait_recv()
        on_to_x(t)
    remote(x_recv, x_recv, ax_ssem, ax_rsem, (dp, mp)).wait_recv()

    for c in range(NCHUNK):
        for xl in range(2):
            cols = slice((2 * c + xl) * 128, (2 * c + xl + 1) * 128)
            for xh in range(2):
                for t in range(NZ):
                    first = xh * 32 + t * 4
                    p_full[first:first + 4, cols] = gathered[t, 2 * xh + xl, :, c * 128:(c + 1) * 128]
    p_high, p_low = split(p_full[...])
    p_out[:RANK, :] = p_high
    p_out[RANK:, :] = p_low
    mh[256:256 + RANK, :] = p_high
    ml[256:256 + RANK, :] = p_low

    both = dot(p_out[...], mh[...], ((1,), (1,)))
    t_local = both[:RANK] + both[RANK:] + dot(p_out[:RANK, :], ml[...], ((1,), (1,)))
    for j in range(NMP):
        t_send[j] = t_local[4 * j:4 * j + 4]

    def scatter_t(k, carry):
        to = (mp + k) % NMP
        remote(t_send.at[to], t_recv.at[k - 1], ts_sem, tr_sem, (dp, to)).start()
        return carry

    lax.fori_loop(1, NMP, scatter_t, 0)
    remote(x_recv, x_recv, ax_ssem, ax_rsem, (dp, mp)).wait_send()
    remote(z_recv, z_recv, az_ssem, az_rsem.at[1], (dp, mp)).wait_send()
    remote(t_recv, t_recv, ts_sem, tr_sem, (dp, mp)).wait_recv()
    slice_sum = t_send[mp]
    for k in range(NMP - 1):
        slice_sum = slice_sum + t_recv[k]
    t_all[dp] = slice_sum[:, :256]
    t_part[...] = slice_sum[:, :256]
    g_gather[mp] = slice_sum[:, 256:]

    def spread_t(k, carry):
        to = (dp + k) % NDP
        remote(t_part, t_all.at[dp], ta_ssem, ta_rsem, (to, mp)).start()
        return carry

    def gather_g(k, carry):
        remote(g_gather.at[mp], g_gather.at[mp], gg_ssem, gg_rsem, (dp, (mp + k) % NMP)).start()
        return carry

    lax.fori_loop(1, NMP, gather_g, 0)
    lax.fori_loop(1, NDP, spread_t, 0)
    rest_g = g_gather.at[pl.ds(0, NMP - 1)]
    remote(rest_g, rest_g, gg_ssem, gg_rsem, (dp, mp)).wait_recv()
    for j in range(NMP):
        g_full[4 * j:4 * j + 4, :] = g_gather[j]
    remote(t_recv, t_recv, ts_sem, tr_sem, (dp, mp)).wait_send()
    remote(rest_g, rest_g, gg_ssem, gg_rsem, (dp, mp)).wait_send()

    rest_t = t_all.at[pl.ds(0, NDP - 1)]
    remote(rest_t, rest_t, ta_ssem, ta_rsem, (dp, mp)).wait_recv()
    total = t_all[0]
    for k in range(1, NDP):
        total = total + t_all[k]
    t_gather[mp] = total

    def gather_t(k, carry):
        remote(t_gather.at[mp], t_gather.at[mp], tg_ssem, tg_rsem, (dp, (mp + k) % NMP)).start()
        return carry

    lax.fori_loop(1, NMP, gather_t, 0)
    remote(rest_t, rest_t, ta_ssem, ta_rsem, (dp, mp)).wait_send()
    inverse = inverse_factor(g_full[...])
    rest_s = t_gather.at[pl.ds(0, NMP - 1)]
    remote(rest_s, rest_s, tg_ssem, tg_rsem, (dp, mp)).wait_recv()
    for j in range(NMP):
        t_full[4 * j:4 * j + 4, :] = t_gather[j]
    exact = lax.Precision.HIGHEST
    q_next = lax.dot_general(
        t_full[...].T * (1.0 / NDP), inverse, (((1,), (1,)), ((), ())),
        precision=exact, preferred_element_type=F32,
    )[:COLS]
    q_out[...] = q_next
    v_out[...] = lax.dot_general(
        q_next, inverse, (((1,), (0,)), ((), ())), precision=exact, preferred_element_type=F32
    )
    remote(rest_s, rest_s, tg_ssem, tg_rsem, (dp, mp)).wait_send()


def output_kernel(g_ref, e_ref, p_ref, v_ref, q_ref, u_out, e_out, q_out):
    @pl.when(pl.program_id(0) == 0)
    def _():
        q_out[0] = q_ref[...]

    v_high, v_low = split(v_ref[...])
    left = jnp.concatenate([v_high, v_low, v_high], axis=1)
    p_high = p_ref[:RANK, :]
    right = jnp.concatenate([p_high, p_high, p_ref[RANK:, :]], axis=0)
    update = dot(left, right, ((1,), (0,)))
    u_out[...] = update.astype(BF16)
    e_out[0] = g_ref[0].astype(F32) + e_ref[0] - update


def on_device(gradients, errors, q_start):
    vmem = pl.BlockSpec(memory_space=pltpu.VMEM)
    hbm = pl.BlockSpec(memory_space=pl.ANY)
    dma, reg = pltpu.SemaphoreType.DMA, pltpu.SemaphoreType.REGULAR
    p_both, v, q_next = pl.pallas_call(
        round_kernel,
        name="power_round",
        out_shape=(
            jax.ShapeDtypeStruct((2 * RANK, FL), BF16),
            jax.ShapeDtypeStruct((COLS, RANK), F32),
            jax.ShapeDtypeStruct((COLS, RANK), F32),
        ),
        in_specs=[hbm, hbm, vmem],
        out_specs=(vmem, vmem, vmem),
        scratch_shapes=[
            pltpu.VMEM((COLS, FL), BF16),
            pltpu.VMEM((COLS, FL), F32),
            pltpu.VMEM((ROWS_T, FL), BF16),
            pltpu.VMEM((ROWS_T, FL), BF16),
            pltpu.VMEM((NZ, NX, 4, HALF), F32),
            pltpu.VMEM((NZ, NX - 1, 4, HALF), F32),
            pltpu.VMEM((NZ, 4, HALF), F32),
            pltpu.VMEM((NZ - 1, 4, HALF), F32),
            pltpu.VMEM((NZ, NX, 4, HALF), F32),
            pltpu.VMEM((RANK, FL), F32),
            pltpu.VMEM((NMP, 4, ROWS_T), F32),
            pltpu.VMEM((NMP - 1, 4, ROWS_T), F32),
            pltpu.VMEM((4, 256), F32),
            pltpu.VMEM((NDP, 4, 256), F32),
            pltpu.VMEM((NMP, 4, 256), F32),
            pltpu.VMEM((NMP, 4, 128), F32),
            pltpu.VMEM((RANK, 256), F32),
            pltpu.VMEM((RANK, 128), F32),
            dma((NCHUNK, 2)),
            dma, dma((NZ,)), dma, dma, dma, dma((NZ,)), dma, dma,
            dma, dma, dma, dma, dma, dma, dma, dma,
        ],
        compiler_params=pltpu.CompilerParams(
            collective_id=0, has_side_effects=True, vmem_limit_bytes=40 << 20
        ),
    )(gradients, errors, q_start)

    def columns(*lead):
        return pl.BlockSpec(lead + (CHUNK,), lambda i: (0,) * len(lead) + (i,))

    def whole(*shape):
        return pl.BlockSpec(shape, lambda i: (0,) * len(shape))

    return pl.pallas_call(
        output_kernel,
        name="outputs",
        grid=(NCHUNK,),
        out_shape=(
            jax.ShapeDtypeStruct((COLS, FL), BF16),
            jax.ShapeDtypeStruct((1, COLS, FL), F32),
            jax.ShapeDtypeStruct((1, COLS, RANK), F32),
        ),
        in_specs=[
            columns(1, COLS), columns(1, COLS), columns(2 * RANK),
            whole(COLS, RANK), whole(COLS, RANK),
        ],
        out_specs=(columns(COLS), columns(1, COLS), whole(1, COLS, RANK)),
        compiler_params=pltpu.CompilerParams(vmem_limit_bytes=32 << 20),
    )(gradients, errors, p_both, v, q_next)


def solution(mesh):
    return jax.shard_map(
        on_device,
        mesh=mesh,
        in_specs=(P("dp", None, "mp"), P("dp", None, "mp"), P()),
        out_specs=(P(None, "mp"), P("dp", None, "mp"), P()),
        check_vma=False,
    )
```

time: 345 us -> 66.2 us (0.19)
  waiting for transfers between devices: 160 us -> 0 us
  blocking collectives: 145 us -> 0 us
  Pallas kernels: 0 us -> 61 us
  between operations: 14.1 us -> 0.65 us
  other arithmetic: 12.1 us -> 0 us
  matrix products: 12 us -> 0 us
    psum x1 -> x0, waiting for transfers between devices: 160 us -> none  [power_round(): p_mean = lax.psum(local_p, 'dp') / replicas]
    psum x2 -> x0, blocking collectives: 145 us -> none  [the longest x1 98.1 us: power_round(): q_total = lax.psum(q_local, ('dp', 'mp'))]
    pallas_call x0 -> x2, Pallas kernels: none -> 61 us  [the longest x1 57 us: on_device(): pl.pallas_call(round_kernel, name='power_round', out_shape=(jax.ShapeDtyp...]
    another operation x5 -> x0, other arithmetic: 12.1 us -> none  [the longest x3 6.52 us: orthonormal_rows(): lower = jnp.linalg.cholesky(gram_sum)]
    dot_general x4 -> x0, matrix products: 10.4 us -> none  [the longest x1 3.84 us: power_round(): local_p = jnp.einsum('kdf,kdr->krf', blocks, q_old, precision=highest)]
  transfers between devices with their start and end apart: 1 -> 0, of which waited for: 1 -> 0; matrix products, arithmetic and copies ran while one was open for 0% -> 0% of each run, Pallas kernels for 0% -> 0%
where the time goes in v1:
time: 66.2 us; the launch traced here: 66 us
  Pallas kernels  61 us (92%)
  local copies, waits for them, and re-layouts  4.26 us (6%)
    pallas_call x1, Pallas kernels, on_device(): pl.pallas_call(round_kernel, name='power_round', out_shape=(jax.ShapeDtyp...  57 us
    pallas_call x1, Pallas kernels, on_device(): pl.pallas_call(output_kernel, name='outputs', grid=(NCHUNK,), out_shape=(...  4.05 us
    unnamed x5, local copies, waits for them, and re-layouts  3.55 us

profile of v1, /device:TPU:1, one launch (start us, length us, event | category | flops | bytes accessed | tf_op | source)
XLA Modules:
  0.0 66.0 jit_solution(7334601067913517048)
XLA Ops:
  0.6 0.9 %copy.6.q_ref = f32[1,240,64]{2,1,0:T(8,128)S(1)} copy(f32[1,240,64]{1,2,0:T(8,128)} %param.5) | data formatting | bytes 122880 | tf_op args[2]
  1.6 0.0 copy-start
  1.6 1.5 %copy-done = f32[1,240,1792]{2,1,0:T(8,128)S(1)} copy-done((f32[1,240,1792]{2,1,0:T(8,128)S(1)}, f32[1,240,1792]{2,1,0:T(8,128)}, u32[]{:S(2)}) %copy-start) | copy-done | bytes 1720344
  3.0 0.0 copy-start.1
  3.0 1.2 %copy-done.1 = bf16[1,240,1792]{2,1,0:T(8,128)(2,1)S(1)} copy-done((bf16[1,240,1792]{2,1,0:T(8,128)(2,1)S(1)}, bf16[1,240,1792]{2,1,0:T(8,128)(2,1)}, u32[]{:S(2)}) %copy-start.1) | copy-done | bytes 860184
  4.2 57.0 %power_round.1 = (bf16[128,1792]{1,0:T(8,128)(2,1)S(1)}, f32[240,64]{1,0:T(8,128)S(1)}, f32[240,64]{1,0:T(8,128)S(1)}) custom-call(bf16[1,240,1792]{2,1,0:T(8,128)(2,1)S(1)} %copy-done.1, f32[1,240,1792]{2,1,0:T(8,128)S(1)} %copy-done, f32[1,240,64]{2,1,0:T(8,128)S(1)} %copy.6.q_ref), custom_call_target="tpu_custom_call" | custom-call | tf_op jit(solution)/shard_map/power_round/pallas_call | solution.py:251
  61.2 4.1 %outputs.1 = (bf16[240,1792]{1,0:T(8,128)(2,1)}, f32[1,240,1792]{2,1,0:T(8,128)}, f32[1,240,64]{2,1,0:T(8,128)S(1)}) custom-call(bf16[1,240,1792]{2,1,0:T(8,128)(2,1)S(1)} %copy-done.1, f32[1,240,1792]{2,1,0:T(8,128)S(1)} %copy-done, bf16[128,1792]{1,0:T(8,128)(2,1)S(1)} %get-tuple-element.6.p_ref, f32[240,64]{1,0:T(8,128)S(1)} %get-tuple-element.7.v_ref, ...), custom_call_target="tpu_custom_call" | custom-call | tf_op jit(solution)/shard_map/outputs/pallas_call | solution.py:295
  65.2 0.7 %copy.7 = f32[1,240,64]{1,2,0:T(8,128)} copy(f32[1,240,64]{2,1,0:T(8,128)S(1)} %get-tuple-element.11) | data formatting | bytes 122880 | tf_op jit(solution)/shard_map/outputs/pallas_call | solution.py:295
Async XLA Ops:
  1.6 1.5 %copy-start = (f32[1,240,1792]{2,1,0:T(8,128)S(1)}, f32[1,240,1792]{2,1,0:T(8,128)}, u32[]{:S(2)}) copy-start(f32[1,240,1792]{2,1,0:T(8,128)} %e_ref.1) | copy-start | bytes 5160964
  3.0 1.2 %copy-start.1 = (bf16[1,240,1792]{2,1,0:T(8,128)(2,1)S(1)}, bf16[1,240,1792]{2,1,0:T(8,128)(2,1)}, u32[]{:S(2)}) copy-start(bf16[1,240,1792]{2,1,0:T(8,128)(2,1)} %g_ref.1) | copy-start | bytes 2580484

commit v2 on v1

v2 whole, which is shorter than its diff:
```python
import jax
import jax.numpy as jnp
from jax import lax
from jax.experimental import pallas as pl
from jax.experimental.pallas import tpu as pltpu
from jax.sharding import PartitionSpec as P

MESH = pl.DeviceIdType.MESH
NX, NZ, NMP = 4, 8, 16
NDP = NX * NZ
COLS, RANK, FL = 240, 64, 1792
CHUNK = 256
NCHUNK = FL // CHUNK
LIMIT = 58 << 20
ROWS_T = 384
F32, BF16 = jnp.float32, jnp.bfloat16
UNITS = FL // 128 * 16
PIECE = UNITS // NDP
NEAR_FIRST = (1, 7, 2, 6, 3, 5, 4)
MP_FAR_FIRST = (9, 8, 7, 10, 11, 6, 5, 12, 13, 4, 3, 14, 15, 2, 1)


def ring(offset, size):
    return min(offset % size, -offset % size)


DP_FAR_FIRST = sorted(
    ((i, j) for i in range(NZ) for j in range(NX) if i or j),
    key=lambda o: (-ring(o[0], NZ) - ring(o[1], NX), -o[0], -o[1]),
)


def split(value):
    high = value.astype(BF16)
    return high, (value - high.astype(F32)).astype(BF16)


def dot(a, b, dims):
    return lax.dot_general(a, b, (dims, ((), ())), preferred_element_type=F32)


def remote(src, dst, send, recv, target):
    return pltpu.make_async_remote_copy(
        src_ref=src, dst_ref=dst, send_sem=send, recv_sem=recv,
        device_id=target, device_id_type=MESH,
    )


def inverse_factor(gram):
    row_at = lax.broadcasted_iota(jnp.int32, (RANK, 2 * RANK), 0)
    col_at = lax.broadcasted_iota(jnp.int32, (RANK, 2 * RANK), 1)
    work = jnp.where(col_at == row_at + RANK, 1.0, gram)
    done = []
    for j in range(RANK):
        base = 8 * (j // 8)
        local = j - base
        pivot = work[local:local + 1, j:j + 1]
        row = work[local:local + 1, :]
        below = lax.broadcasted_iota(jnp.int32, work.shape, 0) > local
        factor = work[:, j:j + 1] / pivot
        work = work - jnp.where(below, factor * row, 0.0)
        if local == 7:
            done.append(work[:8])
            work = work[8:]
    full = jnp.concatenate(done, axis=0)
    diagonal = jnp.sum(jnp.where(col_at == row_at, full, 0.0), axis=1, keepdims=True)
    return (full / jnp.sqrt(diagonal))[:, RANK:]


def round_kernel(g_hbm, e_hbm, q_hbm, m_hbm, p_out, v_out, q_out,
                 g_buf, e_buf, q_buf, m_buf, mh, ml, local_p, x_recv, z_send, z_recv, gathered, p_full,
                 t_send, t_recv, t_part, t_all, t_gather, g_gather, t_full, g_full,
                 load_sem, q_sem, m_sem, x_ssem, x_rsem, z_ssem, z_rsem, az_ssem, az_rsem, ax_ssem, ax_rsem,
                 ts_sem, tr_sem, ta_ssem, ta_rsem, tg_ssem, tg_rsem, gg_ssem, gg_rsem):
    dp = lax.axis_index("dp")
    mp = lax.axis_index("mp")
    z, x = dp // NX, dp % NX

    def place(i):
        c = (z + i) % NCHUNK
        return c, pl.ds(pl.multiple_of(c * CHUNK, CHUNK), CHUNK)

    def load(i):
        cols = place(i)[1]
        return (
            pltpu.make_async_copy(g_hbm.at[0, :, cols], g_buf.at[i], load_sem.at[i, 0]),
            pltpu.make_async_copy(e_hbm.at[0, :, cols], e_buf.at[i], load_sem.at[i, 1]),
        )

    q_copy = pltpu.make_async_copy(q_hbm, q_buf, q_sem)
    q_copy.start()
    for i in range(NCHUNK):
        for copy in load(i):
            copy.start()

    barrier = pltpu.get_barrier_semaphore()

    def greet_dp(k, carry):
        pl.semaphore_signal(barrier, inc=1, device_id=((dp + k) % NDP, mp), device_id_type=MESH)
        return carry

    def greet_mp(k, carry):
        pl.semaphore_signal(barrier, inc=1, device_id=(dp, (mp + k) % NMP), device_id_type=MESH)
        return carry

    lax.fori_loop(1, NDP, greet_dp, 0)
    lax.fori_loop(1, NMP, greet_mp, 0)

    mh[COLS:256, :] = jnp.zeros((256 - COLS, FL), BF16)
    ml[COLS:256, :] = jnp.zeros((256 - COLS, FL), BF16)
    mh[256 + RANK:, :] = jnp.zeros((ROWS_T - 256 - RANK, FL), BF16)
    ml[256 + RANK:, :] = jnp.zeros((ROWS_T - 256 - RANK, FL), BF16)
    q_copy.wait()
    q_high, q_low = split(q_buf[0])
    q_both = jnp.concatenate([q_high, q_low], axis=0)

    def piece(t, to):
        return pl.ds((t * NX + to) * PIECE, PIECE)

    def send_x(k):
        t = (z + 1 + k) % NZ
        for i in (2, 1, 3):
            to = (x + i) % NX
            remote(local_p.at[piece(t, to)], x_recv.at[t, i - 1], x_ssem, x_rsem.at[t], (z * NX + to, mp)).start()

    for i in range(NCHUNK):
        c, cols = place(i)
        for copy in load(i):
            copy.wait()
        merged = g_buf[i].astype(F32) + e_buf[i]
        m_buf[i] = merged
        high, low = split(merged)
        mh[:COLS, cols] = high
        ml[:COLS, cols] = low
        both = dot(q_both, high, ((1,), (0,)))
        part = both[:RANK] + both[RANK:] + dot(q_high, low, ((1,), (0,)))
        for j in range(CHUNK // 128):
            for group in range(RANK // 4):
                unit = part[4 * group:4 * group + 4, 128 * j:128 * (j + 1)]
                local_p[c * 32 + (j * 16 + group)] = unit
        if i == 0:
            pl.semaphore_wait(barrier, NDP - 1 + NMP - 1)
        else:
            send_x(i - 1)
    send_x(NCHUNK - 1)
    send_x(NCHUNK)
    for i in range(NCHUNK):
        pltpu.make_async_copy(m_buf.at[i], m_hbm.at[:, place(i)[1]], m_sem).start()

    for k in range(NZ):
        t = (z + 1 + k) % NZ
        remote(x_recv.at[t], x_recv.at[t], x_ssem, x_rsem.at[t], (dp, mp)).wait_recv()
        z_send[k] = local_p[piece(t, x)] + x_recv[t, 0] + x_recv[t, 1] + x_recv[t, 2]
        if k < NZ - 1:
            remote(z_send.at[k], z_recv.at[k], z_ssem, z_rsem, (t * NX + x, mp)).start()
    remote(z_recv, z_recv, z_ssem, z_rsem, (dp, mp)).wait_recv()
    mean = z_send[NZ - 1]
    for k in range(NZ - 1):
        mean = mean + z_recv[k]
    gathered[piece(z, x)] = mean * (1.0 / NDP)

    for k in NEAR_FIRST:
        remote(gathered.at[piece(z, x)], gathered.at[piece(z, x)], az_ssem, az_rsem.at[k], ((z + k) % NZ * NX + x, mp)).start()

    def on_to_x(t):
        for i in range(1, NX):
            remote(gathered.at[piece(t, x)], gathered.at[piece(t, x)], ax_ssem, ax_rsem, (z * NX + (x + i) % NX, mp)).start()

    on_to_x(z)
    remote(x_recv, x_recv, x_ssem, x_rsem.at[0], (dp, mp)).wait_send()
    remote(z_recv, z_recv, z_ssem, z_rsem, (dp, mp)).wait_send()
    for k in NEAR_FIRST:
        t = (z + NZ - k) % NZ
        remote(gathered.at[piece(t, x)], gathered.at[piece(t, x)], az_ssem, az_rsem.at[k], (dp, mp)).wait_recv()
        on_to_x(t)
    remote(x_recv, x_recv, ax_ssem, ax_rsem, (dp, mp)).wait_recv()

    for j in range(FL // 128):
        for group in range(RANK // 4):
            p_full[4 * group:4 * group + 4, 128 * j:128 * (j + 1)] = gathered[16 * j + group]
    p_high, p_low = split(p_full[...])
    p_out[:RANK, :] = p_high
    p_out[RANK:, :] = p_low
    mh[256:256 + RANK, :] = p_high
    ml[256:256 + RANK, :] = p_low

    both = dot(p_out[...], mh[...], ((1,), (1,)))
    t_local = both[:RANK] + both[RANK:] + dot(p_out[:RANK, :], ml[...], ((1,), (1,)))
    for j in range(NMP):
        t_send[j] = t_local[4 * j:4 * j + 4]

    for k in MP_FAR_FIRST:
        to = (mp + k) % NMP
        remote(t_send.at[to], t_recv.at[k - 1], ts_sem, tr_sem, (dp, to)).start()
    remote(x_recv, x_recv, ax_ssem, ax_rsem, (dp, mp)).wait_send()
    remote(z_recv, z_recv, az_ssem, az_rsem.at[1], (dp, mp)).wait_send()
    remote(t_recv, t_recv, ts_sem, tr_sem, (dp, mp)).wait_recv()
    slice_sum = t_send[mp]
    for k in range(NMP - 1):
        slice_sum = slice_sum + t_recv[k]
    t_all[dp] = slice_sum[:, :256]
    t_part[...] = slice_sum[:, :256]
    g_gather[mp] = slice_sum[:, 256:]

    for i, j in DP_FAR_FIRST:
        to = (z + i) % NZ * NX + (x + j) % NX
        remote(t_part, t_all.at[dp], ta_ssem, ta_rsem, (to, mp)).start()
    for k in MP_FAR_FIRST:
        remote(g_gather.at[mp], g_gather.at[mp], gg_ssem, gg_rsem, (dp, (mp + k) % NMP)).start()
    rest_g = g_gather.at[pl.ds(0, NMP - 1)]
    remote(rest_g, rest_g, gg_ssem, gg_rsem, (dp, mp)).wait_recv()
    for j in range(NMP):
        g_full[4 * j:4 * j + 4, :] = g_gather[j]
    remote(t_recv, t_recv, ts_sem, tr_sem, (dp, mp)).wait_send()
    remote(rest_g, rest_g, gg_ssem, gg_rsem, (dp, mp)).wait_send()

    rest_t = t_all.at[pl.ds(0, NDP - 1)]
    remote(rest_t, rest_t, ta_ssem, ta_rsem, (dp, mp)).wait_recv()
    total = t_all[0]
    for k in range(1, NDP):
        total = total + t_all[k]
    t_gather[mp] = total

    for k in MP_FAR_FIRST:
        remote(t_gather.at[mp], t_gather.at[mp], tg_ssem, tg_rsem, (dp, (mp + k) % NMP)).start()
    remote(rest_t, rest_t, ta_ssem, ta_rsem, (dp, mp)).wait_send()
    inverse = inverse_factor(g_full[...])
    rest_s = t_gather.at[pl.ds(0, NMP - 1)]
    remote(rest_s, rest_s, tg_ssem, tg_rsem, (dp, mp)).wait_recv()
    for j in range(NMP):
        t_full[4 * j:4 * j + 4, :] = t_gather[j]
    exact = lax.Precision.HIGHEST
    q_rows = lax.dot_general(
        inverse, t_full[...] * (1.0 / NDP), (((1,), (0,)), ((), ())),
        precision=exact, preferred_element_type=F32,
    )[:, :COLS]
    q_out[0] = q_rows
    v_out[...] = lax.dot_general(
        q_rows, inverse, (((0,), (0,)), ((), ())), precision=exact, preferred_element_type=F32
    )
    remote(rest_s, rest_s, tg_ssem, tg_rsem, (dp, mp)).wait_send()
    pltpu.make_async_copy(m_hbm, m_hbm, m_sem).wait()


def output_kernel(m_hbm, p_hbm, v_hbm, q_hbm, u_hbm, e_hbm, q_out,
                  m_buf, p_buf, v_buf, u_buf, e_buf, load_sem, small_sem, store_sem):
    small = (
        pltpu.make_async_copy(v_hbm, v_buf, small_sem.at[0]),
        pltpu.make_async_copy(p_hbm, p_buf, small_sem.at[1]),
    )
    for copy in small:
        copy.start()

    def load(c):
        cols = pl.ds(c * CHUNK, CHUNK)
        return pltpu.make_async_copy(m_hbm.at[:, cols], m_buf.at[:, cols], load_sem.at[c])

    for c in range(NCHUNK):
        load(c).start()
    q_copy = pltpu.make_async_copy(q_hbm, q_out, small_sem.at[2])
    q_copy.start()
    for copy in small:
        copy.wait()
    v_high, v_low = split(v_buf[...])
    left = jnp.concatenate([v_high, v_low, v_high], axis=1)

    def store(c):
        cols = pl.ds(c * CHUNK, CHUNK)
        return (
            pltpu.make_async_copy(u_buf.at[:, cols], u_hbm.at[:, cols], store_sem.at[c, 0]),
            pltpu.make_async_copy(e_buf.at[:, cols], e_hbm.at[0, :, cols], store_sem.at[c, 1]),
        )

    for c in range(NCHUNK):
        cols = slice(c * CHUNK, (c + 1) * CHUNK)
        p_high = p_buf[:RANK, cols]
        right = jnp.concatenate([p_high, p_high, p_buf[RANK:, cols]], axis=0)
        update = dot(left, right, ((1,), (0,)))
        load(c).wait()
        u_buf[:, cols] = update.astype(BF16)
        e_buf[:, cols] = m_buf[:, cols] - update
        for copy in store(c):
            copy.start()
    q_copy.wait()
    for c in range(NCHUNK):
        for copy in store(c):
            copy.wait()


def on_device(gradients, errors, q_start):
    vmem = pl.BlockSpec(memory_space=pltpu.VMEM)
    hbm = pl.BlockSpec(memory_space=pl.ANY)
    dma, reg = pltpu.SemaphoreType.DMA, pltpu.SemaphoreType.REGULAR
    merged, p_both, v, q_rows = pl.pallas_call(
        round_kernel,
        name="power_round",
        out_shape=(
            jax.ShapeDtypeStruct((COLS, FL), F32),
            jax.ShapeDtypeStruct((2 * RANK, FL), BF16),
            jax.ShapeDtypeStruct((COLS, RANK), F32),
            jax.ShapeDtypeStruct((1, RANK, COLS), F32),
        ),
        in_specs=[hbm, hbm, hbm],
        out_specs=(hbm, vmem, vmem, vmem),
        scratch_shapes=[
            pltpu.VMEM((NCHUNK, COLS, CHUNK), BF16),
            pltpu.VMEM((NCHUNK, COLS, CHUNK), F32),
            pltpu.VMEM((1, RANK, COLS), F32),
            pltpu.VMEM((NCHUNK, COLS, CHUNK), F32),
            pltpu.VMEM((ROWS_T, FL), BF16),
            pltpu.VMEM((ROWS_T, FL), BF16),
            pltpu.VMEM((UNITS, 4, 128), F32),
            pltpu.VMEM((NZ, NX - 1, PIECE, 4, 128), F32),
            pltpu.VMEM((NZ, PIECE, 4, 128), F32),
            pltpu.VMEM((NZ - 1, PIECE, 4, 128), F32),
            pltpu.VMEM((UNITS, 4, 128), F32),
            pltpu.VMEM((RANK, FL), F32),
            pltpu.VMEM((NMP, 4, ROWS_T), F32),
            pltpu.VMEM((NMP - 1, 4, ROWS_T), F32),
            pltpu.VMEM((4, 256), F32),
            pltpu.VMEM((NDP, 4, 256), F32),
            pltpu.VMEM((NMP, 4, 256), F32),
            pltpu.VMEM((NMP, 4, 128), F32),
            pltpu.VMEM((RANK, 256), F32),
            pltpu.VMEM((RANK, 128), F32),
            dma((NCHUNK, 2)), dma, dma,
            dma, dma((NZ,)), dma, dma, dma, dma((NZ,)), dma, dma,
            dma, dma, dma, dma, dma, dma, dma, dma,
        ],
        compiler_params=pltpu.CompilerParams(
            collective_id=0, has_side_effects=True, vmem_limit_bytes=LIMIT
        ),
    )(gradients, errors, jnp.swapaxes(q_start, 1, 2))

    update_grad, new_errors, q_rows = pl.pallas_call(
        output_kernel,
        name="outputs",
        out_shape=(
            jax.ShapeDtypeStruct((COLS, FL), BF16),
            jax.ShapeDtypeStruct((1, COLS, FL), F32),
            jax.ShapeDtypeStruct((1, RANK, COLS), F32),
        ),
        in_specs=[hbm, hbm, hbm, hbm],
        out_specs=(hbm, hbm, hbm),
        scratch_shapes=[
            pltpu.VMEM((COLS, FL), F32),
            pltpu.VMEM((2 * RANK, FL), BF16),
            pltpu.VMEM((COLS, RANK), F32),
            pltpu.VMEM((COLS, FL), BF16),
            pltpu.VMEM((COLS, FL), F32),
            dma((NCHUNK,)), dma((3,)), dma((NCHUNK, 2)),
        ],
        compiler_params=pltpu.CompilerParams(vmem_limit_bytes=LIMIT),
    )(merged, p_both, v, q_rows)
    return update_grad, new_errors, jnp.swapaxes(q_rows, 1, 2)


def solution(mesh):
    return jax.shard_map(
        on_device,
        mesh=mesh,
        in_specs=(P("dp", None, "mp"), P("dp", None, "mp"), P()),
        out_specs=(P(None, "mp"), P("dp", None, "mp"), P()),
        check_vma=False,
    )
```

time: 66.2 us -> 60.3 us (0.911)
  local copies, waits for them, and re-layouts: 4.26 us -> 0 us
  Pallas kernels: 61 us -> 59.4 us
    unnamed x5 -> x0, local copies, waits for them, and re-layouts: 3.55 us -> none
    pallas_call x1, Pallas kernels: 57 us -> 55.4 us  [on_device(): pl.pallas_call(round_kernel, name='power_round', out_shape=(jax.ShapeDtyp...]
    pallas_call x1 -> x0, local copies, waits for them, and re-layouts: 0.71 us -> none  [on_device(): pl.pallas_call(output_kernel, name='outputs', grid=(NCHUNK,), out_shape=(...]
where the time goes in v2:
time: 60.3 us; the launch traced here: 60.1 us
  Pallas kernels  59.4 us (99%)
  between operations  0.64 us (1%)
    pallas_call x1, Pallas kernels, on_device(): pl.pallas_call(round_kernel, name='power_round', out_shape=(jax.ShapeDtyp...  55.4 us
    pallas_call x1, Pallas kernels, on_device(): pl.pallas_call(output_kernel, name='outputs', out_shape=(jax.ShapeDtypeSt...  4.06 us

profile of v2, /device:TPU:1, one launch (start us, length us, event | category | flops | bytes accessed | tf_op | source)
XLA Modules:
  0.0 60.1 jit_solution(391599399012140584)
XLA Ops:
  0.6 55.4 %power_round.1 = (f32[240,1792]{1,0:T(8,128)}, bf16[128,1792]{1,0:T(8,128)(2,1)}, f32[240,64]{1,0:T(8,128)}, f32[1,64,240]{2,1,0:T(8,128)}) custom-call(bf16[1,240,1792]{2,1,0:T(8,128)(2,1)} %g_hbm.1, f32[1,240,1792]{2,1,0:T(8,128)} %e_hbm.1, f32[1,64,240]{2,1,0:T(8,128)} %bitcast.2), custom_call_target="tpu_custom_call" | custom-call | tf_op jit(solution)/shard_map/power_round/pallas_call | solution.py:294
  56.0 4.1 %outputs.1 = (bf16[240,1792]{1,0:T(8,128)(2,1)}, f32[1,240,1792]{2,1,0:T(8,128)}, f32[1,64,240]{2,1,0:T(8,128)}) custom-call(f32[240,1792]{1,0:T(8,128)} %get-tuple-element.10.m_hbm, bf16[128,1792]{1,0:T(8,128)(2,1)} %get-tuple-element.11.p_hbm, f32[240,64]{1,0:T(8,128)} %get-tuple-element.12.v_hbm, f32[1,64,240]{2,1,0:T(8,128)} %get-tuple-element.13.q_hbm), custom_call_target="tpu_custom_call" | custom-call | tf_op jit(solution)/shard_map/outputs/pallas_call | solution.py:335

commit v3 on v2

--- a/solution.py
+++ b/solution.py
@@ -11,7 +11,7 @@
 COLS, RANK, FL = 240, 64, 1792
 CHUNK = 256
 NCHUNK = FL // CHUNK
-LIMIT = 58 << 20
+LIMIT = 30 << 20
 ROWS_T = 384
 F32, BF16 = jnp.float32, jnp.bfloat16
 UNITS = FL // 128 * 16
@@ -67,10 +67,10 @@
     return (full / jnp.sqrt(diagonal))[:, RANK:]
 
 
-def round_kernel(g_hbm, e_hbm, q_hbm, m_hbm, p_out, v_out, q_out,
-                 g_buf, e_buf, q_buf, m_buf, mh, ml, local_p, x_recv, z_send, z_recv, gathered, p_full,
+def round_kernel(g_hbm, e_hbm, q_hbm, m_out, p_out, v_out, q_out,
+                 g_buf, e_buf, q_buf, mh, ml, local_p, x_recv, z_send, z_recv, gathered, p_full,
                  t_send, t_recv, t_part, t_all, t_gather, g_gather, t_full, g_full,
-                 load_sem, q_sem, m_sem, x_ssem, x_rsem, z_ssem, z_rsem, az_ssem, az_rsem, ax_ssem, ax_rsem,
+                 load_sem, q_sem, x_ssem, x_rsem, z_ssem, z_rsem, az_ssem, az_rsem, ax_ssem, ax_rsem,
                  ts_sem, tr_sem, ta_ssem, ta_rsem, tg_ssem, tg_rsem, gg_ssem, gg_rsem):
     dp = lax.axis_index("dp")
     mp = lax.axis_index("mp")
@@ -106,10 +106,9 @@
     lax.fori_loop(1, NDP, greet_dp, 0)
     lax.fori_loop(1, NMP, greet_mp, 0)
 
+    t_send[:, :, 256 + RANK:] = jnp.zeros((NMP, 4, ROWS_T - 256 - RANK), F32)
     mh[COLS:256, :] = jnp.zeros((256 - COLS, FL), BF16)
     ml[COLS:256, :] = jnp.zeros((256 - COLS, FL), BF16)
-    mh[256 + RANK:, :] = jnp.zeros((ROWS_T - 256 - RANK, FL), BF16)
-    ml[256 + RANK:, :] = jnp.zeros((ROWS_T - 256 - RANK, FL), BF16)
     q_copy.wait()
     q_high, q_low = split(q_buf[0])
     q_both = jnp.concatenate([q_high, q_low], axis=0)
@@ -128,7 +127,7 @@
         for copy in load(i):
             copy.wait()
         merged = g_buf[i].astype(F32) + e_buf[i]
-        m_buf[i] = merged
+        m_out[:, cols] = merged
         high, low = split(merged)
         mh[:COLS, cols] = high
         ml[:COLS, cols] = low
@@ -144,8 +143,6 @@
             send_x(i - 1)
     send_x(NCHUNK - 1)
     send_x(NCHUNK)
-    for i in range(NCHUNK):
-        pltpu.make_async_copy(m_buf.at[i], m_hbm.at[:, place(i)[1]], m_sem).start()
 
     for k in range(NZ):
         t = (z + 1 + k) % NZ
@@ -181,13 +178,13 @@
     p_high, p_low = split(p_full[...])
     p_out[:RANK, :] = p_high
     p_out[RANK:, :] = p_low
-    mh[256:256 + RANK, :] = p_high
-    ml[256:256 + RANK, :] = p_low
-
     both = dot(p_out[...], mh[...], ((1,), (1,)))
     t_local = both[:RANK] + both[RANK:] + dot(p_out[:RANK, :], ml[...], ((1,), (1,)))
+    both = dot(p_out[...], p_out[...], ((1,), (1,)))
+    g_local = both[:RANK, :RANK] + both[:RANK, RANK:] + both[RANK:, :RANK]
     for j in range(NMP):
-        t_send[j] = t_local[4 * j:4 * j + 4]
+        t_send[j, :, :256] = t_local[4 * j:4 * j + 4]
+        t_send[j, :, 256:256 + RANK] = g_local[4 * j:4 * j + 4]
 
     for k in MP_FAR_FIRST:
         to = (mp + k) % NMP
@@ -239,29 +236,10 @@
         q_rows, inverse, (((0,), (0,)), ((), ())), precision=exact, preferred_element_type=F32
     )
     remote(rest_s, rest_s, tg_ssem, tg_rsem, (dp, mp)).wait_send()
-    pltpu.make_async_copy(m_hbm, m_hbm, m_sem).wait()
-
-
-def output_kernel(m_hbm, p_hbm, v_hbm, q_hbm, u_hbm, e_hbm, q_out,
-                  m_buf, p_buf, v_buf, u_buf, e_buf, load_sem, small_sem, store_sem):
-    small = (
-        pltpu.make_async_copy(v_hbm, v_buf, small_sem.at[0]),
-        pltpu.make_async_copy(p_hbm, p_buf, small_sem.at[1]),
-    )
-    for copy in small:
-        copy.start()
-
-    def load(c):
-        cols = pl.ds(c * CHUNK, CHUNK)
-        return pltpu.make_async_copy(m_hbm.at[:, cols], m_buf.at[:, cols], load_sem.at[c])
-
-    for c in range(NCHUNK):
-        load(c).start()
-    q_copy = pltpu.make_async_copy(q_hbm, q_out, small_sem.at[2])
-    q_copy.start()
-    for copy in small:
-        copy.wait()
-    v_high, v_low = split(v_buf[...])
+
+
+def output_kernel(m_ref, p_ref, v_ref, q_ref, u_hbm, e_hbm, q_out, u_buf, e_buf, store_sem):
+    v_high, v_low = split(v_ref[...])
     left = jnp.concatenate([v_high, v_low, v_high], axis=1)
 
     def store(c):
@@ -273,15 +251,14 @@
 
     for c in range(NCHUNK):
         cols = slice(c * CHUNK, (c + 1) * CHUNK)
-        p_high = p_buf[:RANK, cols]
-        right = jnp.concatenate([p_high, p_high, p_buf[RANK:, cols]], axis=0)
+        p_high = p_ref[:RANK, cols]
+        right = jnp.concatenate([p_high, p_high, p_ref[RANK:, cols]], axis=0)
         update = dot(left, right, ((1,), (0,)))
-        load(c).wait()
         u_buf[:, cols] = update.astype(BF16)
-        e_buf[:, cols] = m_buf[:, cols] - update
+        e_buf[:, cols] = m_ref[:, cols] - update
         for copy in store(c):
             copy.start()
-    q_copy.wait()
+    q_out[...] = q_ref[...]
     for c in range(NCHUNK):
         for copy in store(c):
             copy.wait()
@@ -301,14 +278,13 @@
             jax.ShapeDtypeStruct((1, RANK, COLS), F32),
         ),
         in_specs=[hbm, hbm, hbm],
-        out_specs=(hbm, vmem, vmem, vmem),
+        out_specs=(vmem, vmem, vmem, vmem),
         scratch_shapes=[
             pltpu.VMEM((NCHUNK, COLS, CHUNK), BF16),
             pltpu.VMEM((NCHUNK, COLS, CHUNK), F32),
             pltpu.VMEM((1, RANK, COLS), F32),
-            pltpu.VMEM((NCHUNK, COLS, CHUNK), F32),
-            pltpu.VMEM((ROWS_T, FL), BF16),
-            pltpu.VMEM((ROWS_T, FL), BF16),
+            pltpu.VMEM((256, FL), BF16),
+            pltpu.VMEM((256, FL), BF16),
             pltpu.VMEM((UNITS, 4, 128), F32),
             pltpu.VMEM((NZ, NX - 1, PIECE, 4, 128), F32),
             pltpu.VMEM((NZ, PIECE, 4, 128), F32),
@@ -323,14 +299,14 @@
             pltpu.VMEM((NMP, 4, 128), F32),
             pltpu.VMEM((RANK, 256), F32),
             pltpu.VMEM((RANK, 128), F32),
-            dma((NCHUNK, 2)), dma, dma,
+            dma((NCHUNK, 2)), dma,
             dma, dma((NZ,)), dma, dma, dma, dma((NZ,)), dma, dma,
             dma, dma, dma, dma, dma, dma, dma, dma,
         ],
         compiler_params=pltpu.CompilerParams(
             collective_id=0, has_side_effects=True, vmem_limit_bytes=LIMIT
         ),
-    )(gradients, errors, jnp.swapaxes(q_start, 1, 2))
+    )(*(pltpu.with_memory_space_constraint(a, pltpu.HBM) for a in (gradients, errors, jnp.swapaxes(q_start, 1, 2))))
 
     update_grad, new_errors, q_rows = pl.pallas_call(
         output_kernel,
@@ -340,15 +316,12 @@
             jax.ShapeDtypeStruct((1, COLS, FL), F32),
             jax.ShapeDtypeStruct((1, RANK, COLS), F32),
         ),
-        in_specs=[hbm, hbm, hbm, hbm],
-        out_specs=(hbm, hbm, hbm),
+        in_specs=[vmem, vmem, vmem, vmem],
+        out_specs=(hbm, hbm, vmem),
         scratch_shapes=[
-            pltpu.VMEM((COLS, FL), F32),
-            pltpu.VMEM((2 * RANK, FL), BF16),
-            pltpu.VMEM((COLS, RANK), F32),
             pltpu.VMEM((COLS, FL), BF16),
             pltpu.VMEM((COLS, FL), F32),
-            dma((NCHUNK,)), dma((3,)), dma((NCHUNK, 2)),
+            dma((NCHUNK, 2)),
         ],
         compiler_params=pltpu.CompilerParams(vmem_limit_bytes=LIMIT),
     )(merged, p_both, v, q_rows)

time: 60.3 us -> 57.7 us (0.957)
  Pallas kernels: 59.4 us -> 56.9 us
    pallas_call x1, Pallas kernels: 4.06 us -> 2.46 us  [on_device(): pl.pallas_call(output_kernel, name='outputs', out_shape=(jax.ShapeDtypeSt...]
    pallas_call x1, Pallas kernels: 55.4 us -> 54.5 us  [on_device(): pl.pallas_call(round_kernel, name='power_round', out_shape=(jax.ShapeDtyp...]
where the time goes in v3:
time: 57.7 us; the launch traced here: 57.6 us
  Pallas kernels  56.9 us (99%)
  between operations  0.64 us (1%)
    pallas_call x1, Pallas kernels, on_device(): pl.pallas_call(round_kernel, name='power_round', out_shape=(jax.ShapeDtyp...  54.5 us
    pallas_call x1, Pallas kernels, on_device(): pl.pallas_call(output_kernel, name='outputs', out_shape=(jax.ShapeDtypeSt...  2.46 us

profile of v3, /device:TPU:1, one launch (start us, length us, event | category | flops | bytes accessed | tf_op | source)
XLA Modules:
  0.0 57.6 jit_solution(9684184089342151094)
XLA Ops:
  0.6 54.5 %power_round.1 = (f32[240,1792]{1,0:T(8,128)S(1)}, bf16[128,1792]{1,0:T(8,128)(2,1)S(1)}, f32[240,64]{1,0:T(8,128)S(1)}, f32[1,64,240]{2,1,0:T(8,128)S(1)}) custom-call(bf16[1,240,1792]{2,1,0:T(8,128)(2,1)} %g_hbm.1, f32[1,240,1792]{2,1,0:T(8,128)} %e_hbm.1, f32[1,64,240]{2,1,0:T(8,128)} %bitcast.2), custom_call_target="tpu_custom_call" | custom-call | tf_op jit(solution)/shard_map/power_round/pallas_call | solution.py:271
  55.1 2.5 %outputs.1 = (bf16[240,1792]{1,0:T(8,128)(2,1)}, f32[1,240,1792]{2,1,0:T(8,128)}, f32[1,64,240]{2,1,0:T(8,128)}) custom-call(f32[240,1792]{1,0:T(8,128)S(1)} %get-tuple-element.10.m_ref, bf16[128,1792]{1,0:T(8,128)(2,1)S(1)} %get-tuple-element.11.p_ref, f32[240,64]{1,0:T(8,128)S(1)} %get-tuple-element.12.v_ref, f32[1,64,240]{2,1,0:T(8,128)S(1)} %get-tuple-element.13.q_ref), custom_call_target="tpu_custom_call" | custom-call | tf_op jit(solution)/shard_map/outputs/pallas_call | solution.py:311

commit v4 on v3

--- a/solution.py
+++ b/solution.py
@@ -1,3 +1,5 @@
+import functools
+
 import jax
 import jax.numpy as jnp
 from jax import lax
@@ -76,6 +78,18 @@
     mp = lax.axis_index("mp")
     z, x = dp // NX, dp % NX
 
+    barrier = pltpu.get_barrier_semaphore()
+
+    def greet(target):
+        pl.semaphore_signal(barrier, inc=1, device_id=target, device_id_type=MESH)
+
+    for k in reversed(NEAR_FIRST):
+        greet(((z + k) % NZ * NX + x, mp))
+    for k in MP_FAR_FIRST:
+        greet((dp, (mp + k) % NMP))
+    for i in (2, 1, 3):
+        greet((z * NX + (x + i) % NX, mp))
+
     def place(i):
         c = (z + i) % NCHUNK
         return c, pl.ds(pl.multiple_of(c * CHUNK, CHUNK), CHUNK)
@@ -93,20 +107,6 @@
         for copy in load(i):
             copy.start()
 
-    barrier = pltpu.get_barrier_semaphore()
-
-    def greet_dp(k, carry):
-        pl.semaphore_signal(barrier, inc=1, device_id=((dp + k) % NDP, mp), device_id_type=MESH)
-        return carry
-
-    def greet_mp(k, carry):
-        pl.semaphore_signal(barrier, inc=1, device_id=(dp, (mp + k) % NMP), device_id_type=MESH)
-        return carry
-
-    lax.fori_loop(1, NDP, greet_dp, 0)
-    lax.fori_loop(1, NMP, greet_mp, 0)
-
-    t_send[:, :, 256 + RANK:] = jnp.zeros((NMP, 4, ROWS_T - 256 - RANK), F32)
     mh[COLS:256, :] = jnp.zeros((256 - COLS, FL), BF16)
     ml[COLS:256, :] = jnp.zeros((256 - COLS, FL), BF16)
     q_copy.wait()
@@ -137,9 +137,9 @@
             for group in range(RANK // 4):
                 unit = part[4 * group:4 * group + 4, 128 * j:128 * (j + 1)]
                 local_p[c * 32 + (j * 16 + group)] = unit
-        if i == 0:
-            pl.semaphore_wait(barrier, NDP - 1 + NMP - 1)
-        else:
+        if i == 1:
+            pl.semaphore_wait(barrier, NX - 1 + NZ - 1 + NMP - 1)
+        if i:
             send_x(i - 1)
     send_x(NCHUNK - 1)
     send_x(NCHUNK)
@@ -161,7 +161,7 @@
 
     def on_to_x(t):
         for i in range(1, NX):
-            remote(gathered.at[piece(t, x)], gathered.at[piece(t, x)], ax_ssem, ax_rsem, (z * NX + (x + i) % NX, mp)).start()
+            remote(gathered.at[piece(t, x)], gathered.at[piece(t, x)], ax_ssem, ax_rsem.at[t], (z * NX + (x + i) % NX, mp)).start()
 
     on_to_x(z)
     remote(x_recv, x_recv, x_ssem, x_rsem.at[0], (dp, mp)).wait_send()
@@ -170,26 +170,38 @@
         t = (z + NZ - k) % NZ
         remote(gathered.at[piece(t, x)], gathered.at[piece(t, x)], az_ssem, az_rsem.at[k], (dp, mp)).wait_recv()
         on_to_x(t)
-    remote(x_recv, x_recv, ax_ssem, ax_rsem, (dp, mp)).wait_recv()
-
-    for j in range(FL // 128):
-        for group in range(RANK // 4):
-            p_full[4 * group:4 * group + 4, 128 * j:128 * (j + 1)] = gathered[16 * j + group]
-    p_high, p_low = split(p_full[...])
-    p_out[:RANK, :] = p_high
-    p_out[RANK:, :] = p_low
-    both = dot(p_out[...], mh[...], ((1,), (1,)))
-    t_local = both[:RANK] + both[RANK:] + dot(p_out[:RANK, :], ml[...], ((1,), (1,)))
-    both = dot(p_out[...], p_out[...], ((1,), (1,)))
-    g_local = both[:RANK, :RANK] + both[:RANK, RANK:] + both[RANK:, :RANK]
+
+    def accumulate(c):
+        cols = pl.ds(pl.multiple_of(c * CHUNK, CHUNK), CHUNK)
+        for j in range(CHUNK // 128):
+            for group in range(RANK // 4):
+                p_full[4 * group:4 * group + 4, 128 * j:128 * (j + 1)] = gathered[c * 32 + (j * 16 + group)]
+        p_high, p_low = split(p_full[...])
+        p_out[:RANK, cols] = p_high
+        p_out[RANK:, cols] = p_low
+        p_both = jnp.concatenate([p_high, p_low], axis=0)
+        both = dot(p_both, mh[:, cols], ((1,), (1,)))
+        t_full[...] += both[:RANK] + both[RANK:] + dot(p_high, ml[:, cols], ((1,), (1,)))
+        both = dot(p_both, p_both, ((1,), (1,)))
+        g_full[:, :RANK] += both[:RANK, :RANK] + both[:RANK, RANK:] + both[RANK:, :RANK]
+
+    t_full[...] = jnp.zeros_like(t_full)
+    g_full[...] = jnp.zeros_like(g_full)
+    for k, chunks in ((0, ()), (1, (0,)), (7, (7,)), (2, (1,)), (6, (6,)), (3, (2,)), (5, (5,)), (4, (3, 4))):
+        t = (z + k) % NZ
+        remote(x_recv.at[t], x_recv.at[t], ax_ssem, ax_rsem.at[t], (dp, mp)).wait_recv()
+        for o in chunks:
+            c = (z + o) % NZ
+            pl.when(c < NCHUNK)(functools.partial(accumulate, c))
+
     for j in range(NMP):
-        t_send[j, :, :256] = t_local[4 * j:4 * j + 4]
-        t_send[j, :, 256:256 + RANK] = g_local[4 * j:4 * j + 4]
+        t_send[j, :, :256] = t_full[4 * j:4 * j + 4, :]
+        t_send[j, :, 256:] = g_full[4 * j:4 * j + 4, :]
 
     for k in MP_FAR_FIRST:
         to = (mp + k) % NMP
         remote(t_send.at[to], t_recv.at[k - 1], ts_sem, tr_sem, (dp, to)).start()
-    remote(x_recv, x_recv, ax_ssem, ax_rsem, (dp, mp)).wait_send()
+    remote(x_recv, x_recv, ax_ssem, ax_rsem.at[0], (dp, mp)).wait_send()
     remote(z_recv, z_recv, az_ssem, az_rsem.at[1], (dp, mp)).wait_send()
     remote(t_recv, t_recv, ts_sem, tr_sem, (dp, mp)).wait_recv()
     slice_sum = t_send[mp]
@@ -290,7 +302,7 @@
             pltpu.VMEM((NZ, PIECE, 4, 128), F32),
             pltpu.VMEM((NZ - 1, PIECE, 4, 128), F32),
             pltpu.VMEM((UNITS, 4, 128), F32),
-            pltpu.VMEM((RANK, FL), F32),
+            pltpu.VMEM((RANK, CHUNK), F32),
             pltpu.VMEM((NMP, 4, ROWS_T), F32),
             pltpu.VMEM((NMP - 1, 4, ROWS_T), F32),
             pltpu.VMEM((4, 256), F32),
@@ -300,7 +312,7 @@
             pltpu.VMEM((RANK, 256), F32),
             pltpu.VMEM((RANK, 128), F32),
             dma((NCHUNK, 2)), dma,
-            dma, dma((NZ,)), dma, dma, dma, dma((NZ,)), dma, dma,
+            dma, dma((NZ,)), dma, dma, dma, dma((NZ,)), dma, dma((NZ,)),
             dma, dma, dma, dma, dma, dma, dma, dma,
         ],
         compiler_params=pltpu.CompilerParams(

time: 57.7 us -> 56.3 us (0.976)
  Pallas kernels: 56.9 us -> 55.5 us
    pallas_call x1, Pallas kernels: 54.5 us -> 53.1 us  [on_device(): pl.pallas_call(round_kernel, name='power_round', out_shape=(jax.ShapeDtyp...]
where the time goes in v4:
time: 56.3 us; the launch traced here: 56.2 us
  Pallas kernels  55.5 us (99%)
  between operations  0.64 us (1%)
    pallas_call x1, Pallas kernels, on_device(): pl.pallas_call(round_kernel, name='power_round', out_shape=(jax.ShapeDtyp...  53.1 us
    pallas_call x1, Pallas kernels, on_device(): pl.pallas_call(output_kernel, name='outputs', out_shape=(jax.ShapeDtypeSt...  2.46 us

profile of v4, /device:TPU:1, one launch (start us, length us, event | category | flops | bytes accessed | tf_op | source)
XLA Modules:
  0.0 56.2 jit_solution(3375204390870839285)
XLA Ops:
  0.6 53.1 %power_round.1 = (f32[240,1792]{1,0:T(8,128)S(1)}, bf16[128,1792]{1,0:T(8,128)(2,1)S(1)}, f32[240,64]{1,0:T(8,128)S(1)}, f32[1,64,240]{2,1,0:T(8,128)S(1)}) custom-call(bf16[1,240,1792]{2,1,0:T(8,128)(2,1)} %g_hbm.1, f32[1,240,1792]{2,1,0:T(8,128)} %e_hbm.1, f32[1,64,240]{2,1,0:T(8,128)} %bitcast.2), custom_call_target="tpu_custom_call" | custom-call | tf_op jit(solution)/shard_map/power_round/pallas_call | solution.py:283
  53.7 2.5 %outputs.1 = (bf16[240,1792]{1,0:T(8,128)(2,1)}, f32[1,240,1792]{2,1,0:T(8,128)}, f32[1,64,240]{2,1,0:T(8,128)}) custom-call(f32[240,1792]{1,0:T(8,128)S(1)} %get-tuple-element.10.m_ref, bf16[128,1792]{1,0:T(8,128)(2,1)S(1)} %get-tuple-element.11.p_ref, f32[240,64]{1,0:T(8,128)S(1)} %get-tuple-element.12.v_ref, f32[1,64,240]{2,1,0:T(8,128)S(1)} %get-tuple-element.13.q_ref), custom_call_target="tpu_custom_call" | custom-call | tf_op jit(solution)/shard_map/outputs/pallas_call | solution.py:323

commit v5 on v4

--- a/solution.py
+++ b/solution.py
@@ -14,10 +14,11 @@
 CHUNK = 256
 NCHUNK = FL // CHUNK
 LIMIT = 30 << 20
-ROWS_T = 384
 F32, BF16 = jnp.float32, jnp.bfloat16
 UNITS = FL // 128 * 16
-PIECE = UNITS // NDP
+BLOCK = UNITS // NZ
+PIECE = 6
+REST = NX * PIECE
 NEAR_FIRST = (1, 7, 2, 6, 3, 5, 4)
 MP_FAR_FIRST = (9, 8, 7, 10, 11, 6, 5, 12, 13, 4, 3, 14, 15, 2, 1)
 
@@ -70,10 +71,11 @@
 
 
 def round_kernel(g_hbm, e_hbm, q_hbm, m_out, p_out, v_out, q_out,
-                 g_buf, e_buf, q_buf, mh, ml, local_p, x_recv, z_send, z_recv, gathered, p_full,
-                 t_send, t_recv, t_part, t_all, t_gather, g_gather, t_full, g_full,
+                 g_buf, e_buf, q_buf, mh, ml, local_p, x_recv, z_send, z_recv, zb_recv, b_send, xb_recv, gathered, p_full,
+                 t_send, t_recv, g_send, g_recv, t_part, t_all, t_gather, g_gather, t_full, g_full,
                  load_sem, q_sem, x_ssem, x_rsem, z_ssem, z_rsem, az_ssem, az_rsem, ax_ssem, ax_rsem,
-                 ts_sem, tr_sem, ta_ssem, ta_rsem, tg_ssem, tg_rsem, gg_ssem, gg_rsem):
+                 zb_ssem, zb_rsem, xb_ssem, xb_rsem, xg_ssem, xg_rsem, bz_ssem, bz_rsem,
+                 ts_sem, tr_sem, gs_sem, gr_sem, ta_ssem, ta_rsem, tg_ssem, tg_rsem, gg_ssem, gg_rsem):
     dp = lax.axis_index("dp")
     mp = lax.axis_index("mp")
     z, x = dp // NX, dp % NX
@@ -114,13 +116,18 @@
     q_both = jnp.concatenate([q_high, q_low], axis=0)
 
     def piece(t, to):
-        return pl.ds((t * NX + to) * PIECE, PIECE)
+        return pl.ds(t * BLOCK + to * PIECE, PIECE)
+
+    def rest(t):
+        return pl.ds(t * BLOCK + REST, NX)
 
     def send_x(k):
         t = (z + 1 + k) % NZ
         for i in (2, 1, 3):
             to = (x + i) % NX
             remote(local_p.at[piece(t, to)], x_recv.at[t, i - 1], x_ssem, x_rsem.at[t], (z * NX + to, mp)).start()
+        if k < NZ - 1:
+            remote(local_p.at[rest(t)], zb_recv.at[k], zb_ssem, zb_rsem, (t * NX + x, mp)).start()
 
     for i in range(NCHUNK):
         c, cols = place(i)
@@ -150,6 +157,15 @@
         z_send[k] = local_p[piece(t, x)] + x_recv[t, 0] + x_recv[t, 1] + x_recv[t, 2]
         if k < NZ - 1:
             remote(z_send.at[k], z_recv.at[k], z_ssem, z_rsem, (t * NX + x, mp)).start()
+        if k == 4:
+            remote(zb_recv, zb_recv, zb_ssem, zb_rsem, (dp, mp)).wait_recv()
+            total = local_p[rest(z)]
+            for j in range(NZ - 1):
+                total = total + zb_recv[j]
+            b_send[...] = total
+            for i in (2, 1, 3):
+                to = (x + i) % NX
+                remote(b_send.at[to], xb_recv.at[i - 1], xb_ssem, xb_rsem, (z * NX + to, mp)).start()
     remote(z_recv, z_recv, z_ssem, z_rsem, (dp, mp)).wait_recv()
     mean = z_send[NZ - 1]
     for k in range(NZ - 1):
@@ -159,6 +175,14 @@
     for k in NEAR_FIRST:
         remote(gathered.at[piece(z, x)], gathered.at[piece(z, x)], az_ssem, az_rsem.at[k], ((z + k) % NZ * NX + x, mp)).start()
 
+    unit_own = z * BLOCK + REST + x
+    remote(xb_recv, xb_recv, xb_ssem, xb_rsem, (dp, mp)).wait_recv()
+    total = b_send[x] + xb_recv[0] + xb_recv[1] + xb_recv[2]
+    gathered[unit_own] = total * (1.0 / NDP)
+    for i in (2, 1, 3):
+        to = (x + i) % NX
+        remote(gathered.at[unit_own], gathered.at[unit_own], xg_ssem, xg_rsem, (z * NX + to, mp)).start()
+
     def on_to_x(t):
         for i in range(1, NX):
             remote(gathered.at[piece(t, x)], gathered.at[piece(t, x)], ax_ssem, ax_rsem.at[t], (z * NX + (x + i) % NX, mp)).start()
@@ -166,10 +190,17 @@
     on_to_x(z)
     remote(x_recv, x_recv, x_ssem, x_rsem.at[0], (dp, mp)).wait_send()
     remote(z_recv, z_recv, z_ssem, z_rsem, (dp, mp)).wait_send()
+    remote(zb_recv, zb_recv, zb_ssem, zb_rsem, (dp, mp)).wait_send()
+    remote(xb_recv, xb_recv, xb_ssem, xb_rsem, (dp, mp)).wait_send()
     for k in NEAR_FIRST:
         t = (z + NZ - k) % NZ
         remote(gathered.at[piece(t, x)], gathered.at[piece(t, x)], az_ssem, az_rsem.at[k], (dp, mp)).wait_recv()
         on_to_x(t)
+        if k == 7:
+            remote(xb_recv, xb_recv, xg_ssem, xg_rsem, (dp, mp)).wait_recv()
+            for j in reversed(NEAR_FIRST):
+                remote(gathered.at[rest(z)], gathered.at[rest(z)], bz_ssem, bz_rsem.at[j],
+                       ((z + j) % NZ * NX + x, mp)).start()
 
     def accumulate(c):
         cols = pl.ds(pl.multiple_of(c * CHUNK, CHUNK), CHUNK)
@@ -190,30 +221,41 @@
     for k, chunks in ((0, ()), (1, (0,)), (7, (7,)), (2, (1,)), (6, (6,)), (3, (2,)), (5, (5,)), (4, (3, 4))):
         t = (z + k) % NZ
         remote(x_recv.at[t], x_recv.at[t], ax_ssem, ax_rsem.at[t], (dp, mp)).wait_recv()
+        if k:
+            remote(gathered.at[rest(t)], gathered.at[rest(t)], bz_ssem, bz_rsem.at[NZ - k], (dp, mp)).wait_recv()
         for o in chunks:
             c = (z + o) % NZ
             pl.when(c < NCHUNK)(functools.partial(accumulate, c))
 
     for j in range(NMP):
-        t_send[j, :, :256] = t_full[4 * j:4 * j + 4, :]
-        t_send[j, :, 256:] = g_full[4 * j:4 * j + 4, :]
+        t_send[j] = t_full[4 * j:4 * j + 4, :]
+        g_send[j] = g_full[4 * j:4 * j + 4, :]
 
     for k in MP_FAR_FIRST:
         to = (mp + k) % NMP
         remote(t_send.at[to], t_recv.at[k - 1], ts_sem, tr_sem, (dp, to)).start()
+    for k in MP_FAR_FIRST:
+        to = (mp + k) % NMP
+        remote(g_send.at[to], g_recv.at[k - 1], gs_sem, gr_sem, (dp, to)).start()
+    remote(xb_recv, xb_recv, xg_ssem, xg_rsem, (dp, mp)).wait_send()
+    remote(zb_recv, zb_recv, bz_ssem, bz_rsem.at[1], (dp, mp)).wait_send()
     remote(x_recv, x_recv, ax_ssem, ax_rsem.at[0], (dp, mp)).wait_send()
     remote(z_recv, z_recv, az_ssem, az_rsem.at[1], (dp, mp)).wait_send()
     remote(t_recv, t_recv, ts_sem, tr_sem, (dp, mp)).wait_recv()
     slice_sum = t_send[mp]
     for k in range(NMP - 1):
         slice_sum = slice_sum + t_recv[k]
-    t_all[dp] = slice_sum[:, :256]
-    t_part[...] = slice_sum[:, :256]
-    g_gather[mp] = slice_sum[:, 256:]
+    t_all[dp] = slice_sum
+    t_part[...] = slice_sum
 
     for i, j in DP_FAR_FIRST:
         to = (z + i) % NZ * NX + (x + j) % NX
         remote(t_part, t_all.at[dp], ta_ssem, ta_rsem, (to, mp)).start()
+    remote(g_recv, g_recv, gs_sem, gr_sem, (dp, mp)).wait_recv()
+    slice_sum = g_send[mp]
+    for k in range(NMP - 1):
+        slice_sum = slice_sum + g_recv[k]
+    g_gather[mp] = slice_sum
     for k in MP_FAR_FIRST:
         remote(g_gather.at[mp], g_gather.at[mp], gg_ssem, gg_rsem, (dp, (mp + k) % NMP)).start()
     rest_g = g_gather.at[pl.ds(0, NMP - 1)]
@@ -221,6 +263,7 @@
     for j in range(NMP):
         g_full[4 * j:4 * j + 4, :] = g_gather[j]
     remote(t_recv, t_recv, ts_sem, tr_sem, (dp, mp)).wait_send()
+    remote(g_recv, g_recv, gs_sem, gr_sem, (dp, mp)).wait_send()
     remote(rest_g, rest_g, gg_ssem, gg_rsem, (dp, mp)).wait_send()
 
     rest_t = t_all.at[pl.ds(0, NDP - 1)]
@@ -301,10 +344,15 @@
             pltpu.VMEM((NZ, NX - 1, PIECE, 4, 128), F32),
             pltpu.VMEM((NZ, PIECE, 4, 128), F32),
             pltpu.VMEM((NZ - 1, PIECE, 4, 128), F32),
+            pltpu.VMEM((NZ - 1, NX, 4, 128), F32),
+            pltpu.VMEM((NX, 4, 128), F32),
+            pltpu.VMEM((NX - 1, 4, 128), F32),
             pltpu.VMEM((UNITS, 4, 128), F32),
             pltpu.VMEM((RANK, CHUNK), F32),
-            pltpu.VMEM((NMP, 4, ROWS_T), F32),
-            pltpu.VMEM((NMP - 1, 4, ROWS_T), F32),
+            pltpu.VMEM((NMP, 4, 256), F32),
+            pltpu.VMEM((NMP - 1, 4, 256), F32),
+            pltpu.VMEM((NMP, 4, 128), F32),
+            pltpu.VMEM((NMP - 1, 4, 128), F32),
             pltpu.VMEM((4, 256), F32),
             pltpu.VMEM((NDP, 4, 256), F32),
             pltpu.VMEM((NMP, 4, 256), F32),
@@ -313,6 +361,7 @@
             pltpu.VMEM((RANK, 128), F32),
             dma((NCHUNK, 2)), dma,
             dma, dma((NZ,)), dma, dma, dma, dma((NZ,)), dma, dma((NZ,)),
+            dma, dma, dma, dma, dma, dma, dma, dma((NZ,)), dma, dma,
             dma, dma, dma, dma, dma, dma, dma, dma,
         ],
         compiler_params=pltpu.CompilerParams(

time: 56.3 us -> 56.1 us (level)
  no operation moved by 1% of the time
where the time goes in v5:
time: 56.1 us; the launch traced here: 55.9 us
  Pallas kernels  55.3 us (99%)
  between operations  0.64 us (1%)
    pallas_call x1, Pallas kernels, on_device(): pl.pallas_call(round_kernel, name='power_round', out_shape=(jax.ShapeDtyp...  52.8 us
    pallas_call x1, Pallas kernels, on_device(): pl.pallas_call(output_kernel, name='outputs', out_shape=(jax.ShapeDtypeSt...  2.46 us

profile of v5, /device:TPU:1, one launch (start us, length us, event | category | flops | bytes accessed | tf_op | source)
XLA Modules:
  0.0 55.9 jit_solution(17602802089447191568)
XLA Ops:
  0.6 52.8 %power_round.1 = (f32[240,1792]{1,0:T(8,128)S(1)}, bf16[128,1792]{1,0:T(8,128)(2,1)S(1)}, f32[240,64]{1,0:T(8,128)S(1)}, f32[1,64,240]{2,1,0:T(8,128)S(1)}) custom-call(bf16[1,240,1792]{2,1,0:T(8,128)(2,1)} %g_hbm.1, f32[1,240,1792]{2,1,0:T(8,128)} %e_hbm.1, f32[1,64,240]{2,1,0:T(8,128)} %bitcast.2), custom_call_target="tpu_custom_call" | custom-call | tf_op jit(solution)/shard_map/power_round/pallas_call | solution.py:326
  53.5 2.5 %outputs.1 = (bf16[240,1792]{1,0:T(8,128)(2,1)}, f32[1,240,1792]{2,1,0:T(8,128)}, f32[1,64,240]{2,1,0:T(8,128)}) custom-call(f32[240,1792]{1,0:T(8,128)S(1)} %get-tuple-element.10.m_ref, bf16[128,1792]{1,0:T(8,128)(2,1)S(1)} %get-tuple-element.11.p_ref, f32[240,64]{1,0:T(8,128)S(1)} %get-tuple-element.12.v_ref, f32[1,64,240]{2,1,0:T(8,128)S(1)} %get-tuple-element.13.q_ref), custom_call_target="tpu_custom_call" | custom-call | tf_op jit(solution)/shard_map/outputs/pallas_call | solution.py:372

commit v6 on v5

--- a/solution.py
+++ b/solution.py
@@ -8,7 +8,7 @@
 from jax.sharding import PartitionSpec as P
 
 MESH = pl.DeviceIdType.MESH
-NX, NZ, NMP = 4, 8, 16
+NX, NY, NZ, NMP = 4, 8, 8, 16
 NDP = NX * NZ
 COLS, RANK, FL = 240, 64, 1792
 CHUNK = 256
@@ -72,13 +72,14 @@
 
 def round_kernel(g_hbm, e_hbm, q_hbm, m_out, p_out, v_out, q_out,
                  g_buf, e_buf, q_buf, mh, ml, local_p, x_recv, z_send, z_recv, zb_recv, b_send, xb_recv, gathered, p_full,
-                 t_send, t_recv, g_send, g_recv, t_part, t_all, t_gather, g_gather, t_full, g_full,
+                 t_recv, g_recv, t_part, t_all, t_full, g_full, t_total, g_total,
                  load_sem, q_sem, x_ssem, x_rsem, z_ssem, z_rsem, az_ssem, az_rsem, ax_ssem, ax_rsem,
                  zb_ssem, zb_rsem, xb_ssem, xb_rsem, xg_ssem, xg_rsem, bz_ssem, bz_rsem,
                  ts_sem, tr_sem, gs_sem, gr_sem, ta_ssem, ta_rsem, tg_ssem, tg_rsem, gg_ssem, gg_rsem):
     dp = lax.axis_index("dp")
     mp = lax.axis_index("mp")
     z, x = dp // NX, dp % NX
+    y, core = mp // 2, mp % 2
 
     barrier = pltpu.get_barrier_semaphore()
 
@@ -227,70 +228,91 @@
             c = (z + o) % NZ
             pl.when(c < NCHUNK)(functools.partial(accumulate, c))
 
-    for j in range(NMP):
-        t_send[j] = t_full[4 * j:4 * j + 4, :]
-        g_send[j] = g_full[4 * j:4 * j + 4, :]
-
-    for k in MP_FAR_FIRST:
-        to = (mp + k) % NMP
-        remote(t_send.at[to], t_recv.at[k - 1], ts_sem, tr_sem, (dp, to)).start()
-    for k in MP_FAR_FIRST:
-        to = (mp + k) % NMP
-        remote(g_send.at[to], g_recv.at[k - 1], gs_sem, gr_sem, (dp, to)).start()
+    def rows(at):
+        return pl.ds(pl.multiple_of(at * 8, 8), 8)
+
+    def to_owner(ref, recv, ssem, rsem, k):
+        owner = (y + k) % NY
+        remote(ref.at[rows(owner)], recv.at[2 * k + core], ssem, rsem, (dp, 2 * owner)).start()
+
+    for ref, recv, ssem, rsem in ((t_full, t_recv, ts_sem, tr_sem), (g_full, g_recv, gs_sem, gr_sem)):
+        for k in reversed(NEAR_FIRST):
+            to_owner(ref, recv, ssem, rsem, k)
+        pl.when(core == 1)(functools.partial(to_owner, ref, recv, ssem, rsem, 0))
     remote(xb_recv, xb_recv, xg_ssem, xg_rsem, (dp, mp)).wait_send()
     remote(zb_recv, zb_recv, bz_ssem, bz_rsem.at[1], (dp, mp)).wait_send()
     remote(x_recv, x_recv, ax_ssem, ax_rsem.at[0], (dp, mp)).wait_send()
     remote(z_recv, z_recv, az_ssem, az_rsem.at[1], (dp, mp)).wait_send()
-    remote(t_recv, t_recv, ts_sem, tr_sem, (dp, mp)).wait_recv()
-    slice_sum = t_send[mp]
-    for k in range(NMP - 1):
-        slice_sum = slice_sum + t_recv[k]
-    t_all[dp] = slice_sum
-    t_part[...] = slice_sum
-
-    for i, j in DP_FAR_FIRST:
-        to = (z + i) % NZ * NX + (x + j) % NX
-        remote(t_part, t_all.at[dp], ta_ssem, ta_rsem, (to, mp)).start()
-    remote(g_recv, g_recv, gs_sem, gr_sem, (dp, mp)).wait_recv()
-    slice_sum = g_send[mp]
-    for k in range(NMP - 1):
-        slice_sum = slice_sum + g_recv[k]
-    g_gather[mp] = slice_sum
-    for k in MP_FAR_FIRST:
-        remote(g_gather.at[mp], g_gather.at[mp], gg_ssem, gg_rsem, (dp, (mp + k) % NMP)).start()
-    rest_g = g_gather.at[pl.ds(0, NMP - 1)]
-    remote(rest_g, rest_g, gg_ssem, gg_rsem, (dp, mp)).wait_recv()
-    for j in range(NMP):
-        g_full[4 * j:4 * j + 4, :] = g_gather[j]
-    remote(t_recv, t_recv, ts_sem, tr_sem, (dp, mp)).wait_send()
-    remote(g_recv, g_recv, gs_sem, gr_sem, (dp, mp)).wait_send()
-    remote(rest_g, rest_g, gg_ssem, gg_rsem, (dp, mp)).wait_send()
-
-    rest_t = t_all.at[pl.ds(0, NDP - 1)]
-    remote(rest_t, rest_t, ta_ssem, ta_rsem, (dp, mp)).wait_recv()
-    total = t_all[0]
-    for k in range(1, NDP):
-        total = total + t_all[k]
-    t_gather[mp] = total
-
-    for k in MP_FAR_FIRST:
-        remote(t_gather.at[mp], t_gather.at[mp], tg_ssem, tg_rsem, (dp, (mp + k) % NMP)).start()
-    remote(rest_t, rest_t, ta_ssem, ta_rsem, (dp, mp)).wait_send()
-    inverse = inverse_factor(g_full[...])
-    rest_s = t_gather.at[pl.ds(0, NMP - 1)]
-    remote(rest_s, rest_s, tg_ssem, tg_rsem, (dp, mp)).wait_recv()
-    for j in range(NMP):
-        t_full[4 * j:4 * j + 4, :] = t_gather[j]
+
+    def own_sum(ref, recv, ssem, rsem):
+        arrived = recv.at[pl.ds(1, NMP - 1)]
+        remote(arrived, arrived, ssem, rsem, (dp, mp)).wait_recv()
+        total = ref[rows(y), :]
+        for k in range(1, NMP):
+            total = total + recv[k]
+        return total
+
+    def to_all(ref, ssem, rsem):
+        for k in MP_FAR_FIRST:
+            remote(ref.at[rows(y)], ref.at[rows(y)], ssem, rsem, (dp, (mp + k) % NMP)).start()
+
+    @pl.when(core == 0)
+    def _():
+        total = own_sum(t_full, t_recv, ts_sem, tr_sem)
+        t_all[dp] = total
+        t_part[...] = total
+        for i, j in DP_FAR_FIRST:
+            to = (z + i) % NZ * NX + (x + j) % NX
+            remote(t_part, t_all.at[dp], ta_ssem, ta_rsem, (to, mp)).start()
+        g_total[rows(y), :] = own_sum(g_full, g_recv, gs_sem, gr_sem)
+        to_all(g_total, gg_ssem, gg_rsem)
+        for sent, ssem, rsem in (
+            (t_full.at[pl.ds(0, 8 * (NY - 1))], ts_sem, tr_sem),
+            (g_full.at[pl.ds(0, 8 * (NY - 1))], gs_sem, gr_sem),
+        ):
+            remote(sent, sent, ssem, rsem, (dp, mp)).wait_send()
+        arrived = t_all.at[pl.ds(0, NDP - 1)]
+        remote(arrived, arrived, ta_ssem, ta_rsem, (dp, mp)).wait_recv()
+        total = t_all[0]
+        for k in range(1, NDP):
+            total = total + t_all[k]
+        t_total[rows(y), :] = total
+        to_all(t_total, tg_ssem, tg_rsem)
+        remote(arrived, arrived, ta_ssem, ta_rsem, (dp, mp)).wait_send()
+
+    @pl.when(core == 1)
+    def _():
+        remote(t_full, t_full, ts_sem, tr_sem, (dp, mp)).wait_send()
+        remote(g_full, g_full, gs_sem, gr_sem, (dp, mp)).wait_send()
+
+    def wait_rows(ref, ssem, rsem):
+        @pl.when(core == 0)
+        def _():
+            others = ref.at[pl.ds(0, 8 * (NY - 1))]
+            remote(others, others, ssem, rsem, (dp, mp)).wait_recv()
+
+        @pl.when(core == 1)
+        def _():
+            remote(ref, ref, ssem, rsem, (dp, mp)).wait_recv()
+
+    wait_rows(g_total, gg_ssem, gg_rsem)
+    inverse = inverse_factor(g_total[...])
+    wait_rows(t_total, tg_ssem, tg_rsem)
     exact = lax.Precision.HIGHEST
     q_rows = lax.dot_general(
-        inverse, t_full[...] * (1.0 / NDP), (((1,), (0,)), ((), ())),
+        inverse, t_total[...] * (1.0 / NDP), (((1,), (0,)), ((), ())),
         precision=exact, preferred_element_type=F32,
     )[:, :COLS]
     q_out[0] = q_rows
     v_out[...] = lax.dot_general(
         q_rows, inverse, (((0,), (0,)), ((), ())), precision=exact, preferred_element_type=F32
     )
-    remote(rest_s, rest_s, tg_ssem, tg_rsem, (dp, mp)).wait_send()
+
+    @pl.when(core == 0)
+    def _():
+        for recv, ssem, rsem in ((g_recv, gg_ssem, gg_rsem), (t_recv, tg_ssem, tg_rsem)):
+            sent = recv.at[pl.ds(1, NMP - 1)]
+            remote(sent, sent, ssem, rsem, (dp, mp)).wait_send()
 
 
 def output_kernel(m_ref, p_ref, v_ref, q_ref, u_hbm, e_hbm, q_out, u_buf, e_buf, store_sem):
@@ -349,14 +371,12 @@
             pltpu.VMEM((NX - 1, 4, 128), F32),
             pltpu.VMEM((UNITS, 4, 128), F32),
             pltpu.VMEM((RANK, CHUNK), F32),
-            pltpu.VMEM((NMP, 4, 256), F32),
-            pltpu.VMEM((NMP - 1, 4, 256), F32),
-            pltpu.VMEM((NMP, 4, 128), F32),
-            pltpu.VMEM((NMP - 1, 4, 128), F32),
-            pltpu.VMEM((4, 256), F32),
-            pltpu.VMEM((NDP, 4, 256), F32),
-            pltpu.VMEM((NMP, 4, 256), F32),
-            pltpu.VMEM((NMP, 4, 128), F32),
+            pltpu.VMEM((NMP, 8, 256), F32),
+            pltpu.VMEM((NMP, 8, 128), F32),
+            pltpu.VMEM((8, 256), F32),
+            pltpu.VMEM((NDP, 8, 256), F32),
+            pltpu.VMEM((RANK, 256), F32),
+            pltpu.VMEM((RANK, 128), F32),
             pltpu.VMEM((RANK, 256), F32),
             pltpu.VMEM((RANK, 128), F32),
             dma((NCHUNK, 2)), dma,

time: 56.1 us -> 56.8 us (1.012)
  Pallas kernels: 55.3 us -> 56 us
    pallas_call x1, Pallas kernels: 52.8 us -> 53.5 us  [on_device(): pl.pallas_call(round_kernel, name='power_round', out_shape=(jax.ShapeDtyp...]
where the time goes in v6:
time: 56.8 us; the launch traced here: 56.6 us
  Pallas kernels  56 us (99%)
  between operations  0.64 us (1%)
    pallas_call x1, Pallas kernels, on_device(): pl.pallas_call(round_kernel, name='power_round', out_shape=(jax.ShapeDtyp...  53.5 us
    pallas_call x1, Pallas kernels, on_device(): pl.pallas_call(output_kernel, name='outputs', out_shape=(jax.ShapeDtypeSt...  2.46 us

profile of v6, /device:TPU:1, one launch (start us, length us, event | category | flops | bytes accessed | tf_op | source)
XLA Modules:
  0.0 56.6 jit_solution(14341850326561405173)
XLA Ops:
  0.6 53.5 %power_round.1 = (f32[240,1792]{1,0:T(8,128)S(1)}, bf16[128,1792]{1,0:T(8,128)(2,1)S(1)}, f32[240,64]{1,0:T(8,128)S(1)}, f32[1,64,240]{2,1,0:T(8,128)S(1)}) custom-call(bf16[1,240,1792]{2,1,0:T(8,128)(2,1)} %g_hbm.1, f32[1,240,1792]{2,1,0:T(8,128)} %e_hbm.1, f32[1,64,240]{2,1,0:T(8,128)} %bitcast.2), custom_call_target="tpu_custom_call" | custom-call | tf_op jit(solution)/shard_map/power_round/pallas_call | solution.py:348
  54.2 2.5 %outputs.1 = (bf16[240,1792]{1,0:T(8,128)(2,1)}, f32[1,240,1792]{2,1,0:T(8,128)}, f32[1,64,240]{2,1,0:T(8,128)}) custom-call(f32[240,1792]{1,0:T(8,128)S(1)} %get-tuple-element.10.m_ref, bf16[128,1792]{1,0:T(8,128)(2,1)S(1)} %get-tuple-element.11.p_ref, f32[240,64]{1,0:T(8,128)S(1)} %get-tuple-element.12.v_ref, f32[1,64,240]{2,1,0:T(8,128)S(1)} %get-tuple-element.13.q_ref), custom_call_target="tpu_custom_call" | custom-call | tf_op jit(solution)/shard_map/outputs/pallas_call | solution.py:392

commit v7 on v6

--- a/solution.py
+++ b/solution.py
@@ -54,17 +54,16 @@
     col_at = lax.broadcasted_iota(jnp.int32, (RANK, 2 * RANK), 1)
     work = jnp.where(col_at == row_at + RANK, 1.0, gram)
     done = []
-    for j in range(RANK):
-        base = 8 * (j // 8)
-        local = j - base
-        pivot = work[local:local + 1, j:j + 1]
-        row = work[local:local + 1, :]
-        below = lax.broadcasted_iota(jnp.int32, work.shape, 0) > local
-        factor = work[:, j:j + 1] / pivot
-        work = work - jnp.where(below, factor * row, 0.0)
-        if local == 7:
-            done.append(work[:8])
-            work = work[8:]
+    for first in range(0, RANK, 8):
+        at = lax.broadcasted_iota(jnp.int32, work.shape, 0)
+        columns = [jnp.broadcast_to(work[:, first + k:first + k + 1], work.shape) for k in range(8)]
+        for k in range(8):
+            factor = jnp.where(at > k, columns[k] * (1.0 / columns[k][k:k + 1, :]), 0.0)
+            for m in range(k + 1, 8):
+                columns[m] = columns[m] - factor * columns[m][k:k + 1, :]
+            work = work - factor * work[k:k + 1, :]
+        done.append(work[:8])
+        work = work[8:]
     full = jnp.concatenate(done, axis=0)
     diagonal = jnp.sum(jnp.where(col_at == row_at, full, 0.0), axis=1, keepdims=True)
     return (full / jnp.sqrt(diagonal))[:, RANK:]

time: 56.8 us -> 56.8 us (level)
  no operation moved by 1% of the time
where the time goes in v7:
time: 56.8 us; the launch traced here: 56.6 us
  Pallas kernels  56 us (99%)
  between operations  0.64 us (1%)
    pallas_call x1, Pallas kernels, on_device(): pl.pallas_call(round_kernel, name='power_round', out_shape=(jax.ShapeDtyp...  53.5 us
    pallas_call x1, Pallas kernels, on_device(): pl.pallas_call(output_kernel, name='outputs', out_shape=(jax.ShapeDtypeSt...  2.46 us

profile of v7, /device:TPU:1, one launch (start us, length us, event | category | flops | bytes accessed | tf_op | source)
XLA Modules:
  0.0 56.6 jit_solution(15584111144215902187)
XLA Ops:
  0.6 53.5 %power_round.1 = (f32[240,1792]{1,0:T(8,128)S(1)}, bf16[128,1792]{1,0:T(8,128)(2,1)S(1)}, f32[240,64]{1,0:T(8,128)S(1)}, f32[1,64,240]{2,1,0:T(8,128)S(1)}) custom-call(bf16[1,240,1792]{2,1,0:T(8,128)(2,1)} %g_hbm.1, f32[1,240,1792]{2,1,0:T(8,128)} %e_hbm.1, f32[1,64,240]{2,1,0:T(8,128)} %bitcast.2), custom_call_target="tpu_custom_call" | custom-call | tf_op jit(solution)/shard_map/power_round/pallas_call | solution.py:347
  54.2 2.5 %outputs.1 = (bf16[240,1792]{1,0:T(8,128)(2,1)}, f32[1,240,1792]{2,1,0:T(8,128)}, f32[1,64,240]{2,1,0:T(8,128)}) custom-call(f32[240,1792]{1,0:T(8,128)S(1)} %get-tuple-element.10.m_ref, bf16[128,1792]{1,0:T(8,128)(2,1)S(1)} %get-tuple-element.11.p_ref, f32[240,64]{1,0:T(8,128)S(1)} %get-tuple-element.12.v_ref, f32[1,64,240]{2,1,0:T(8,128)S(1)} %get-tuple-element.13.q_ref), custom_call_target="tpu_custom_call" | custom-call | tf_op jit(solution)/shard_map/outputs/pallas_call | solution.py:391

commit v8 on v7

--- a/solution.py
+++ b/solution.py
@@ -71,10 +71,10 @@
 
 def round_kernel(g_hbm, e_hbm, q_hbm, m_out, p_out, v_out, q_out,
                  g_buf, e_buf, q_buf, mh, ml, local_p, x_recv, z_send, z_recv, zb_recv, b_send, xb_recv, gathered, p_full,
-                 t_recv, g_recv, t_part, t_all, t_full, g_full, t_total, g_total,
+                 t_recv, t_part, t_all, t_full, t_total, g_total,
                  load_sem, q_sem, x_ssem, x_rsem, z_ssem, z_rsem, az_ssem, az_rsem, ax_ssem, ax_rsem,
                  zb_ssem, zb_rsem, xb_ssem, xb_rsem, xg_ssem, xg_rsem, bz_ssem, bz_rsem,
-                 ts_sem, tr_sem, gs_sem, gr_sem, ta_ssem, ta_rsem, tg_ssem, tg_rsem, gg_ssem, gg_rsem):
+                 ts_sem, tr_sem, gh_ssem, gh_rsem, ta_ssem, ta_rsem, tg_ssem, tg_rsem, gg_ssem, gg_rsem):
     dp = lax.axis_index("dp")
     mp = lax.axis_index("mp")
     z, x = dp // NX, dp % NX
@@ -212,12 +212,11 @@
         p_out[RANK:, cols] = p_low
         p_both = jnp.concatenate([p_high, p_low], axis=0)
         both = dot(p_both, mh[:, cols], ((1,), (1,)))
-        t_full[...] += both[:RANK] + both[RANK:] + dot(p_high, ml[:, cols], ((1,), (1,)))
+        t_full[:, :256] += both[:RANK] + both[RANK:] + dot(p_high, ml[:, cols], ((1,), (1,)))
         both = dot(p_both, p_both, ((1,), (1,)))
-        g_full[:, :RANK] += both[:RANK, :RANK] + both[:RANK, RANK:] + both[RANK:, :RANK]
+        t_full[:, 256:256 + RANK] += both[:RANK, :RANK] + both[:RANK, RANK:] + both[RANK:, :RANK]
 
     t_full[...] = jnp.zeros_like(t_full)
-    g_full[...] = jnp.zeros_like(g_full)
     for k, chunks in ((0, ()), (1, (0,)), (7, (7,)), (2, (1,)), (6, (6,)), (3, (2,)), (5, (5,)), (4, (3, 4))):
         t = (z + k) % NZ
         remote(x_recv.at[t], x_recv.at[t], ax_ssem, ax_rsem.at[t], (dp, mp)).wait_recv()
@@ -230,73 +229,70 @@
     def rows(at):
         return pl.ds(pl.multiple_of(at * 8, 8), 8)
 
-    def to_owner(ref, recv, ssem, rsem, k):
+    def to_owner(k):
         owner = (y + k) % NY
-        remote(ref.at[rows(owner)], recv.at[2 * k + core], ssem, rsem, (dp, 2 * owner)).start()
-
-    for ref, recv, ssem, rsem in ((t_full, t_recv, ts_sem, tr_sem), (g_full, g_recv, gs_sem, gr_sem)):
-        for k in reversed(NEAR_FIRST):
-            to_owner(ref, recv, ssem, rsem, k)
-        pl.when(core == 1)(functools.partial(to_owner, ref, recv, ssem, rsem, 0))
+        remote(t_full.at[rows(owner)], t_recv.at[2 * k + core], ts_sem, tr_sem, (dp, 2 * owner)).start()
+
+    for k in reversed(NEAR_FIRST):
+        to_owner(k)
+    pl.when(core == 1)(functools.partial(to_owner, 0))
     remote(xb_recv, xb_recv, xg_ssem, xg_rsem, (dp, mp)).wait_send()
     remote(zb_recv, zb_recv, bz_ssem, bz_rsem.at[1], (dp, mp)).wait_send()
     remote(x_recv, x_recv, ax_ssem, ax_rsem.at[0], (dp, mp)).wait_send()
     remote(z_recv, z_recv, az_ssem, az_rsem.at[1], (dp, mp)).wait_send()
 
-    def own_sum(ref, recv, ssem, rsem):
-        arrived = recv.at[pl.ds(1, NMP - 1)]
-        remote(arrived, arrived, ssem, rsem, (dp, mp)).wait_recv()
-        total = ref[rows(y), :]
-        for k in range(1, NMP):
-            total = total + recv[k]
-        return total
-
-    def to_all(ref, ssem, rsem):
-        for k in MP_FAR_FIRST:
-            remote(ref.at[rows(y)], ref.at[rows(y)], ssem, rsem, (dp, (mp + k) % NMP)).start()
+    def handed(core_1):
+        return remote(g_total, g_total, gh_ssem, gh_rsem, (dp, core_1))
 
     @pl.when(core == 0)
     def _():
-        total = own_sum(t_full, t_recv, ts_sem, tr_sem)
-        t_all[dp] = total
-        t_part[...] = total
+        arrived = t_recv.at[pl.ds(1, NMP - 1)]
+        remote(arrived, arrived, ts_sem, tr_sem, (dp, mp)).wait_recv()
+        total = t_full[rows(y), :]
+        for k in range(1, NMP):
+            total = total + t_recv[k]
+        t_all[dp] = total[:, :256]
+        t_part[...] = total[:, :256]
+        g_total[rows(y), :] = total[:, 256:]
         for i, j in DP_FAR_FIRST:
             to = (z + i) % NZ * NX + (x + j) % NX
             remote(t_part, t_all.at[dp], ta_ssem, ta_rsem, (to, mp)).start()
-        g_total[rows(y), :] = own_sum(g_full, g_recv, gs_sem, gr_sem)
-        to_all(g_total, gg_ssem, gg_rsem)
-        for sent, ssem, rsem in (
-            (t_full.at[pl.ds(0, 8 * (NY - 1))], ts_sem, tr_sem),
-            (g_full.at[pl.ds(0, 8 * (NY - 1))], gs_sem, gr_sem),
-        ):
-            remote(sent, sent, ssem, rsem, (dp, mp)).wait_send()
+        for k in reversed(NEAR_FIRST):
+            mine = g_total.at[rows(y)]
+            remote(mine, mine, gg_ssem, gg_rsem, (dp, 2 * ((y + k) % NY))).start()
+        sent = t_full.at[pl.ds(0, 8 * (NY - 1))]
+        remote(sent, sent, ts_sem, tr_sem, (dp, mp)).wait_send()
+        others = g_total.at[pl.ds(0, 8 * (NY - 1))]
+        remote(others, others, gg_ssem, gg_rsem, (dp, mp)).wait_recv()
+        handed(mp + 1).start()
         arrived = t_all.at[pl.ds(0, NDP - 1)]
         remote(arrived, arrived, ta_ssem, ta_rsem, (dp, mp)).wait_recv()
         total = t_all[0]
         for k in range(1, NDP):
             total = total + t_all[k]
         t_total[rows(y), :] = total
-        to_all(t_total, tg_ssem, tg_rsem)
+        for k in MP_FAR_FIRST:
+            mine = t_total.at[rows(y)]
+            remote(mine, mine, tg_ssem, tg_rsem, (dp, (mp + k) % NMP)).start()
         remote(arrived, arrived, ta_ssem, ta_rsem, (dp, mp)).wait_send()
+        remote(others, others, gg_ssem, gg_rsem, (dp, mp)).wait_send()
 
     @pl.when(core == 1)
     def _():
         remote(t_full, t_full, ts_sem, tr_sem, (dp, mp)).wait_send()
-        remote(g_full, g_full, gs_sem, gr_sem, (dp, mp)).wait_send()
-
-    def wait_rows(ref, ssem, rsem):
-        @pl.when(core == 0)
-        def _():
-            others = ref.at[pl.ds(0, 8 * (NY - 1))]
-            remote(others, others, ssem, rsem, (dp, mp)).wait_recv()
-
-        @pl.when(core == 1)
-        def _():
-            remote(ref, ref, ssem, rsem, (dp, mp)).wait_recv()
-
-    wait_rows(g_total, gg_ssem, gg_rsem)
+        handed(mp).wait_recv()
+
     inverse = inverse_factor(g_total[...])
-    wait_rows(t_total, tg_ssem, tg_rsem)
+
+    @pl.when(core == 0)
+    def _():
+        others = t_total.at[pl.ds(0, 8 * (NY - 1))]
+        remote(others, others, tg_ssem, tg_rsem, (dp, mp)).wait_recv()
+
+    @pl.when(core == 1)
+    def _():
+        remote(t_total, t_total, tg_ssem, tg_rsem, (dp, mp)).wait_recv()
+
     exact = lax.Precision.HIGHEST
     q_rows = lax.dot_general(
         inverse, t_total[...] * (1.0 / NDP), (((1,), (0,)), ((), ())),
@@ -309,9 +305,9 @@
 
     @pl.when(core == 0)
     def _():
-        for recv, ssem, rsem in ((g_recv, gg_ssem, gg_rsem), (t_recv, tg_ssem, tg_rsem)):
-            sent = recv.at[pl.ds(1, NMP - 1)]
-            remote(sent, sent, ssem, rsem, (dp, mp)).wait_send()
+        sent = t_all.at[pl.ds(0, NMP - 1)]
+        remote(sent, sent, tg_ssem, tg_rsem, (dp, mp)).wait_send()
+        handed(mp).wait_send()
 
 
 def output_kernel(m_ref, p_ref, v_ref, q_ref, u_hbm, e_hbm, q_out, u_buf, e_buf, store_sem):
@@ -370,12 +366,10 @@
             pltpu.VMEM((NX - 1, 4, 128), F32),
             pltpu.VMEM((UNITS, 4, 128), F32),
             pltpu.VMEM((RANK, CHUNK), F32),
-            pltpu.VMEM((NMP, 8, 256), F32),
-            pltpu.VMEM((NMP, 8, 128), F32),
+            pltpu.VMEM((NMP, 8, 384), F32),
             pltpu.VMEM((8, 256), F32),
             pltpu.VMEM((NDP, 8, 256), F32),
-            pltpu.VMEM((RANK, 256), F32),
-            pltpu.VMEM((RANK, 128), F32),
+            pltpu.VMEM((RANK, 384), F32),
             pltpu.VMEM((RANK, 256), F32),
             pltpu.VMEM((RANK, 128), F32),
             dma((NCHUNK, 2)), dma,

time: 56.8 us -> 56.9 us (level)
  no operation moved by 1% of the time
where the time goes in v8:
time: 56.9 us; the launch traced here: 56.8 us
  Pallas kernels  56.1 us (99%)
  between operations  0.64 us (1%)
    pallas_call x1, Pallas kernels, on_device(): pl.pallas_call(round_kernel, name='power_round', out_shape=(jax.ShapeDtyp...  53.7 us
    pallas_call x1, Pallas kernels, on_device(): pl.pallas_call(output_kernel, name='outputs', out_shape=(jax.ShapeDtypeSt...  2.46 us

profile of v8, /device:TPU:1, one launch (start us, length us, event | category | flops | bytes accessed | tf_op | source)
XLA Modules:
  0.0 56.8 jit_solution(2065719940496657026)
XLA Ops:
  0.6 53.7 %power_round.1 = (f32[240,1792]{1,0:T(8,128)S(1)}, bf16[128,1792]{1,0:T(8,128)(2,1)S(1)}, f32[240,64]{1,0:T(8,128)S(1)}, f32[1,64,240]{2,1,0:T(8,128)S(1)}) custom-call(bf16[1,240,1792]{2,1,0:T(8,128)(2,1)} %g_hbm.1, f32[1,240,1792]{2,1,0:T(8,128)} %e_hbm.1, f32[1,64,240]{2,1,0:T(8,128)} %bitcast.2), custom_call_target="tpu_custom_call" | custom-call | tf_op jit(solution)/shard_map/power_round/pallas_call | solution.py:343
  54.3 2.5 %outputs.1 = (bf16[240,1792]{1,0:T(8,128)(2,1)}, f32[1,240,1792]{2,1,0:T(8,128)}, f32[1,64,240]{2,1,0:T(8,128)}) custom-call(f32[240,1792]{1,0:T(8,128)S(1)} %get-tuple-element.10.m_ref, bf16[128,1792]{1,0:T(8,128)(2,1)S(1)} %get-tuple-element.11.p_ref, f32[240,64]{1,0:T(8,128)S(1)} %get-tuple-element.12.v_ref, f32[1,64,240]{2,1,0:T(8,128)S(1)} %get-tuple-element.13.q_ref), custom_call_target="tpu_custom_call" | custom-call | tf_op jit(solution)/shard_map/outputs/pallas_call | solution.py:385

commit v9 on v8

--- a/solution.py
+++ b/solution.py
@@ -71,10 +71,10 @@
 
 def round_kernel(g_hbm, e_hbm, q_hbm, m_out, p_out, v_out, q_out,
                  g_buf, e_buf, q_buf, mh, ml, local_p, x_recv, z_send, z_recv, zb_recv, b_send, xb_recv, gathered, p_full,
-                 t_recv, t_part, t_all, t_full, t_total, g_total,
+                 t_recv, t_part, t_all, t_full, t_total, g_full, g_peer, g_recv, g_total,
                  load_sem, q_sem, x_ssem, x_rsem, z_ssem, z_rsem, az_ssem, az_rsem, ax_ssem, ax_rsem,
                  zb_ssem, zb_rsem, xb_ssem, xb_rsem, xg_ssem, xg_rsem, bz_ssem, bz_rsem,
-                 ts_sem, tr_sem, gh_ssem, gh_rsem, ta_ssem, ta_rsem, tg_ssem, tg_rsem, gg_ssem, gg_rsem):
+                 ts_sem, tr_sem, gh_ssem, gh_rsem, ta_ssem, ta_rsem, tg_ssem, tg_rsem, gg_ssem, gg_rsem, gp_ssem, gp_rsem, gs_ssem, gs_rsem):
     dp = lax.axis_index("dp")
     mp = lax.axis_index("mp")
     z, x = dp // NX, dp % NX
@@ -172,7 +172,7 @@
         mean = mean + z_recv[k]
     gathered[piece(z, x)] = mean * (1.0 / NDP)
 
-    for k in NEAR_FIRST:
+    for k in (1, 7, 4, 2, 6, 3, 5):
         remote(gathered.at[piece(z, x)], gathered.at[piece(z, x)], az_ssem, az_rsem.at[k], ((z + k) % NZ * NX + x, mp)).start()
 
     unit_own = z * BLOCK + REST + x
@@ -184,7 +184,7 @@
         remote(gathered.at[unit_own], gathered.at[unit_own], xg_ssem, xg_rsem, (z * NX + to, mp)).start()
 
     def on_to_x(t):
-        for i in range(1, NX):
+        for i in (2, 1, 3):
             remote(gathered.at[piece(t, x)], gathered.at[piece(t, x)], ax_ssem, ax_rsem.at[t], (z * NX + (x + i) % NX, mp)).start()
 
     on_to_x(z)
@@ -212,11 +212,12 @@
         p_out[RANK:, cols] = p_low
         p_both = jnp.concatenate([p_high, p_low], axis=0)
         both = dot(p_both, mh[:, cols], ((1,), (1,)))
-        t_full[:, :256] += both[:RANK] + both[RANK:] + dot(p_high, ml[:, cols], ((1,), (1,)))
+        t_full[...] += both[:RANK] + both[RANK:] + dot(p_high, ml[:, cols], ((1,), (1,)))
         both = dot(p_both, p_both, ((1,), (1,)))
-        t_full[:, 256:256 + RANK] += both[:RANK, :RANK] + both[:RANK, RANK:] + both[RANK:, :RANK]
+        g_full[:, :RANK] += both[:RANK, :RANK] + both[:RANK, RANK:] + both[RANK:, :RANK]
 
     t_full[...] = jnp.zeros_like(t_full)
+    g_full[...] = jnp.zeros_like(g_full)
     for k, chunks in ((0, ()), (1, (0,)), (7, (7,)), (2, (1,)), (6, (6,)), (3, (2,)), (5, (5,)), (4, (3, 4))):
         t = (z + k) % NZ
         remote(x_recv.at[t], x_recv.at[t], ax_ssem, ax_rsem.at[t], (dp, mp)).wait_recv()
@@ -233,6 +234,13 @@
         owner = (y + k) % NY
         remote(t_full.at[rows(owner)], t_recv.at[2 * k + core], ts_sem, tr_sem, (dp, 2 * owner)).start()
 
+    def own_gram(core_0):
+        return remote(g_full, g_peer, gp_ssem, gp_rsem, (dp, core_0))
+
+    @pl.when(core == 1)
+    def _():
+        own_gram(mp - 1).start()
+
     for k in reversed(NEAR_FIRST):
         to_owner(k)
     pl.when(core == 1)(functools.partial(to_owner, 0))
@@ -246,22 +254,32 @@
 
     @pl.when(core == 0)
     def _():
+        own_gram(mp).wait_recv()
+        g_full[...] += g_peer[...]
+        for k in reversed(NEAR_FIRST):
+            owner = (y + k) % NY
+            remote(g_full.at[rows(owner)], g_recv.at[k - 1], gs_ssem, gs_rsem, (dp, 2 * owner)).start()
         arrived = t_recv.at[pl.ds(1, NMP - 1)]
         remote(arrived, arrived, ts_sem, tr_sem, (dp, mp)).wait_recv()
         total = t_full[rows(y), :]
         for k in range(1, NMP):
             total = total + t_recv[k]
-        t_all[dp] = total[:, :256]
-        t_part[...] = total[:, :256]
-        g_total[rows(y), :] = total[:, 256:]
+        t_all[dp] = total
+        t_part[...] = total
         for i, j in DP_FAR_FIRST:
             to = (z + i) % NZ * NX + (x + j) % NX
             remote(t_part, t_all.at[dp], ta_ssem, ta_rsem, (to, mp)).start()
+        remote(g_recv, g_recv, gs_ssem, gs_rsem, (dp, mp)).wait_recv()
+        total = g_full[rows(y), :]
+        for k in range(NY - 1):
+            total = total + g_recv[k]
+        g_total[rows(y), :] = total
         for k in reversed(NEAR_FIRST):
             mine = g_total.at[rows(y)]
             remote(mine, mine, gg_ssem, gg_rsem, (dp, 2 * ((y + k) % NY))).start()
         sent = t_full.at[pl.ds(0, 8 * (NY - 1))]
         remote(sent, sent, ts_sem, tr_sem, (dp, mp)).wait_send()
+        remote(g_recv, g_recv, gs_ssem, gs_rsem, (dp, mp)).wait_send()
         others = g_total.at[pl.ds(0, 8 * (NY - 1))]
         remote(others, others, gg_ssem, gg_rsem, (dp, mp)).wait_recv()
         handed(mp + 1).start()
@@ -280,6 +298,7 @@
     @pl.when(core == 1)
     def _():
         remote(t_full, t_full, ts_sem, tr_sem, (dp, mp)).wait_send()
+        own_gram(mp).wait_send()
         handed(mp).wait_recv()
 
     inverse = inverse_factor(g_total[...])
@@ -366,16 +385,20 @@
             pltpu.VMEM((NX - 1, 4, 128), F32),
             pltpu.VMEM((UNITS, 4, 128), F32),
             pltpu.VMEM((RANK, CHUNK), F32),
-            pltpu.VMEM((NMP, 8, 384), F32),
+            pltpu.VMEM((NMP, 8, 256), F32),
             pltpu.VMEM((8, 256), F32),
             pltpu.VMEM((NDP, 8, 256), F32),
-            pltpu.VMEM((RANK, 384), F32),
             pltpu.VMEM((RANK, 256), F32),
+            pltpu.VMEM((RANK, 256), F32),
+            pltpu.VMEM((RANK, 128), F32),
+            pltpu.VMEM((RANK, 128), F32),
+            pltpu.VMEM((NY - 1, 8, 128), F32),
             pltpu.VMEM((RANK, 128), F32),
             dma((NCHUNK, 2)), dma,
             dma, dma((NZ,)), dma, dma, dma, dma((NZ,)), dma, dma((NZ,)),
             dma, dma, dma, dma, dma, dma, dma, dma((NZ,)), dma, dma,
             dma, dma, dma, dma, dma, dma, dma, dma,
+            dma, dma, dma, dma,
         ],
         compiler_params=pltpu.CompilerParams(
             collective_id=0, has_side_effects=True, vmem_limit_bytes=LIMIT

time: 56.9 us -> 56.8 us (level)
  no operation moved by 1% of the time
where the time goes in v9:
time: 56.8 us; the launch traced here: 56.6 us
  Pallas kernels  56 us (99%)
  between operations  0.64 us (1%)
    pallas_call x1, Pallas kernels, on_device(): pl.pallas_call(round_kernel, name='power_round', out_shape=(jax.ShapeDtyp...  53.5 us
    pallas_call x1, Pallas kernels, on_device(): pl.pallas_call(output_kernel, name='outputs', out_shape=(jax.ShapeDtypeSt...  2.46 us

profile of v9, /device:TPU:1, one launch (start us, length us, event | category | flops | bytes accessed | tf_op | source)
XLA Modules:
  0.0 56.6 jit_solution(571947888563649197)
XLA Ops:
  0.6 53.5 %power_round.1 = (f32[240,1792]{1,0:T(8,128)S(1)}, bf16[128,1792]{1,0:T(8,128)(2,1)S(1)}, f32[240,64]{1,0:T(8,128)S(1)}, f32[1,64,240]{2,1,0:T(8,128)S(1)}) custom-call(bf16[1,240,1792]{2,1,0:T(8,128)(2,1)} %g_hbm.1, f32[1,240,1792]{2,1,0:T(8,128)} %e_hbm.1, f32[1,64,240]{2,1,0:T(8,128)} %bitcast.2), custom_call_target="tpu_custom_call" | custom-call | tf_op jit(solution)/shard_map/power_round/pallas_call | solution.py:362
  54.1 2.5 %outputs.1 = (bf16[240,1792]{1,0:T(8,128)(2,1)}, f32[1,240,1792]{2,1,0:T(8,128)}, f32[1,64,240]{2,1,0:T(8,128)}) custom-call(f32[240,1792]{1,0:T(8,128)S(1)} %get-tuple-element.10.m_ref, bf16[128,1792]{1,0:T(8,128)(2,1)S(1)} %get-tuple-element.11.p_ref, f32[240,64]{1,0:T(8,128)S(1)} %get-tuple-element.12.v_ref, f32[1,64,240]{2,1,0:T(8,128)S(1)} %get-tuple-element.13.q_ref), custom_call_target="tpu_custom_call" | custom-call | tf_op jit(solution)/shard_map/outputs/pallas_call | solution.py:408

commit v10 on v5

--- a/solution.py
+++ b/solution.py
@@ -54,17 +54,16 @@
     col_at = lax.broadcasted_iota(jnp.int32, (RANK, 2 * RANK), 1)
     work = jnp.where(col_at == row_at + RANK, 1.0, gram)
     done = []
-    for j in range(RANK):
-        base = 8 * (j // 8)
-        local = j - base
-        pivot = work[local:local + 1, j:j + 1]
-        row = work[local:local + 1, :]
-        below = lax.broadcasted_iota(jnp.int32, work.shape, 0) > local
-        factor = work[:, j:j + 1] / pivot
-        work = work - jnp.where(below, factor * row, 0.0)
-        if local == 7:
-            done.append(work[:8])
-            work = work[8:]
+    for first in range(0, RANK, 8):
+        at = lax.broadcasted_iota(jnp.int32, work.shape, 0)
+        columns = [jnp.broadcast_to(work[:, first + k:first + k + 1], work.shape) for k in range(8)]
+        for k in range(8):
+            factor = jnp.where(at > k, columns[k] * (1.0 / columns[k][k:k + 1, :]), 0.0)
+            for m in range(k + 1, 8):
+                columns[m] = columns[m] - factor * columns[m][k:k + 1, :]
+            work = work - factor * work[k:k + 1, :]
+        done.append(work[:8])
+        work = work[8:]
     full = jnp.concatenate(done, axis=0)
     diagonal = jnp.sum(jnp.where(col_at == row_at, full, 0.0), axis=1, keepdims=True)
     return (full / jnp.sqrt(diagonal))[:, RANK:]

time: 56.1 us -> 56.1 us (level)
  no operation moved by 1% of the time
where the time goes in v10:
time: 56.1 us; the launch traced here: 55.9 us
  Pallas kernels  55.3 us (99%)
  between operations  0.64 us (1%)
    pallas_call x1, Pallas kernels, on_device(): pl.pallas_call(round_kernel, name='power_round', out_shape=(jax.ShapeDtyp...  52.8 us
    pallas_call x1, Pallas kernels, on_device(): pl.pallas_call(output_kernel, name='outputs', out_shape=(jax.ShapeDtypeSt...  2.46 us

profile of v10, /device:TPU:1, one launch (start us, length us, event | category | flops | bytes accessed | tf_op | source)
XLA Modules:
  0.0 55.9 jit_solution(11750409206395624231)
XLA Ops:
  0.6 52.8 %power_round.1 = (f32[240,1792]{1,0:T(8,128)S(1)}, bf16[128,1792]{1,0:T(8,128)(2,1)S(1)}, f32[240,64]{1,0:T(8,128)S(1)}, f32[1,64,240]{2,1,0:T(8,128)S(1)}) custom-call(bf16[1,240,1792]{2,1,0:T(8,128)(2,1)} %g_hbm.1, f32[1,240,1792]{2,1,0:T(8,128)} %e_hbm.1, f32[1,64,240]{2,1,0:T(8,128)} %bitcast.2), custom_call_target="tpu_custom_call" | custom-call | tf_op jit(solution)/shard_map/power_round/pallas_call | solution.py:325
  53.5 2.5 %outputs.1 = (bf16[240,1792]{1,0:T(8,128)(2,1)}, f32[1,240,1792]{2,1,0:T(8,128)}, f32[1,64,240]{2,1,0:T(8,128)}) custom-call(f32[240,1792]{1,0:T(8,128)S(1)} %get-tuple-element.10.m_ref, bf16[128,1792]{1,0:T(8,128)(2,1)S(1)} %get-tuple-element.11.p_ref, f32[240,64]{1,0:T(8,128)S(1)} %get-tuple-element.12.v_ref, f32[1,64,240]{2,1,0:T(8,128)S(1)} %get-tuple-element.13.q_ref), custom_call_target="tpu_custom_call" | custom-call | tf_op jit(solution)/shard_map/outputs/pallas_call | solution.py:371

commit v11 on v10

--- a/solution.py
+++ b/solution.py
@@ -71,10 +71,10 @@
 
 def round_kernel(g_hbm, e_hbm, q_hbm, m_out, p_out, v_out, q_out,
                  g_buf, e_buf, q_buf, mh, ml, local_p, x_recv, z_send, z_recv, zb_recv, b_send, xb_recv, gathered, p_full,
-                 t_send, t_recv, g_send, g_recv, t_part, t_all, t_gather, g_gather, t_full, g_full,
+                 t_send, t_recv, t_part, t_all, t_gather, g_gather, t_full, g_full,
                  load_sem, q_sem, x_ssem, x_rsem, z_ssem, z_rsem, az_ssem, az_rsem, ax_ssem, ax_rsem,
                  zb_ssem, zb_rsem, xb_ssem, xb_rsem, xg_ssem, xg_rsem, bz_ssem, bz_rsem,
-                 ts_sem, tr_sem, gs_sem, gr_sem, ta_ssem, ta_rsem, tg_ssem, tg_rsem, gg_ssem, gg_rsem):
+                 ts_sem, tr_sem, ta_ssem, ta_rsem, tg_ssem, tg_rsem, gg_ssem, gg_rsem):
     dp = lax.axis_index("dp")
     mp = lax.axis_index("mp")
     z, x = dp // NX, dp % NX
@@ -227,15 +227,12 @@
             pl.when(c < NCHUNK)(functools.partial(accumulate, c))
 
     for j in range(NMP):
-        t_send[j] = t_full[4 * j:4 * j + 4, :]
-        g_send[j] = g_full[4 * j:4 * j + 4, :]
+        t_send[j, :, :256] = t_full[4 * j:4 * j + 4, :]
+        t_send[j, :, 256:] = g_full[4 * j:4 * j + 4, :]
 
     for k in MP_FAR_FIRST:
         to = (mp + k) % NMP
         remote(t_send.at[to], t_recv.at[k - 1], ts_sem, tr_sem, (dp, to)).start()
-    for k in MP_FAR_FIRST:
-        to = (mp + k) % NMP
-        remote(g_send.at[to], g_recv.at[k - 1], gs_sem, gr_sem, (dp, to)).start()
     remote(xb_recv, xb_recv, xg_ssem, xg_rsem, (dp, mp)).wait_send()
     remote(zb_recv, zb_recv, bz_ssem, bz_rsem.at[1], (dp, mp)).wait_send()
     remote(x_recv, x_recv, ax_ssem, ax_rsem.at[0], (dp, mp)).wait_send()
@@ -244,26 +241,16 @@
     slice_sum = t_send[mp]
     for k in range(NMP - 1):
         slice_sum = slice_sum + t_recv[k]
-    t_all[dp] = slice_sum
-    t_part[...] = slice_sum
+    t_all[dp] = slice_sum[:, :256]
+    t_part[...] = slice_sum[:, :256]
+    g_gather[mp] = slice_sum[:, 256:]
 
     for i, j in DP_FAR_FIRST:
         to = (z + i) % NZ * NX + (x + j) % NX
         remote(t_part, t_all.at[dp], ta_ssem, ta_rsem, (to, mp)).start()
-    remote(g_recv, g_recv, gs_sem, gr_sem, (dp, mp)).wait_recv()
-    slice_sum = g_send[mp]
-    for k in range(NMP - 1):
-        slice_sum = slice_sum + g_recv[k]
-    g_gather[mp] = slice_sum
     for k in MP_FAR_FIRST:
         remote(g_gather.at[mp], g_gather.at[mp], gg_ssem, gg_rsem, (dp, (mp + k) % NMP)).start()
-    rest_g = g_gather.at[pl.ds(0, NMP - 1)]
-    remote(rest_g, rest_g, gg_ssem, gg_rsem, (dp, mp)).wait_recv()
-    for j in range(NMP):
-        g_full[4 * j:4 * j + 4, :] = g_gather[j]
     remote(t_recv, t_recv, ts_sem, tr_sem, (dp, mp)).wait_send()
-    remote(g_recv, g_recv, gs_sem, gr_sem, (dp, mp)).wait_send()
-    remote(rest_g, rest_g, gg_ssem, gg_rsem, (dp, mp)).wait_send()
 
     rest_t = t_all.at[pl.ds(0, NDP - 1)]
     remote(rest_t, rest_t, ta_ssem, ta_rsem, (dp, mp)).wait_recv()
@@ -275,6 +262,11 @@
     for k in MP_FAR_FIRST:
         remote(t_gather.at[mp], t_gather.at[mp], tg_ssem, tg_rsem, (dp, (mp + k) % NMP)).start()
     remote(rest_t, rest_t, ta_ssem, ta_rsem, (dp, mp)).wait_send()
+    rest_g = g_gather.at[pl.ds(0, NMP - 1)]
+    remote(rest_g, rest_g, gg_ssem, gg_rsem, (dp, mp)).wait_recv()
+    for j in range(NMP):
+        g_full[4 * j:4 * j + 4, :] = g_gather[j]
+    remote(rest_g, rest_g, gg_ssem, gg_rsem, (dp, mp)).wait_send()
     inverse = inverse_factor(g_full[...])
     rest_s = t_gather.at[pl.ds(0, NMP - 1)]
     remote(rest_s, rest_s, tg_ssem, tg_rsem, (dp, mp)).wait_recv()
@@ -348,10 +340,8 @@
             pltpu.VMEM((NX - 1, 4, 128), F32),
             pltpu.VMEM((UNITS, 4, 128), F32),
             pltpu.VMEM((RANK, CHUNK), F32),
-            pltpu.VMEM((NMP, 4, 256), F32),
-            pltpu.VMEM((NMP - 1, 4, 256), F32),
-            pltpu.VMEM((NMP, 4, 128), F32),
-            pltpu.VMEM((NMP - 1, 4, 128), F32),
+            pltpu.VMEM((NMP, 4, 384), F32),
+            pltpu.VMEM((NMP - 1, 4, 384), F32),
             pltpu.VMEM((4, 256), F32),
             pltpu.VMEM((NDP, 4, 256), F32),
             pltpu.VMEM((NMP, 4, 256), F32),
@@ -360,7 +350,7 @@
             pltpu.VMEM((RANK, 128), F32),
             dma((NCHUNK, 2)), dma,
             dma, dma((NZ,)), dma, dma, dma, dma((NZ,)), dma, dma((NZ,)),
-            dma, dma, dma, dma, dma, dma, dma, dma((NZ,)), dma, dma,
+            dma, dma, dma, dma, dma, dma, dma, dma((NZ,)),
             dma, dma, dma, dma, dma, dma, dma, dma,
         ],
         compiler_params=pltpu.CompilerParams(

time: 56.1 us -> 56 us (level)
  no operation moved by 1% of the time
where the time goes in v11:
time: 56 us; the launch traced here: 55.9 us
  Pallas kernels  55.2 us (99%)
  between operations  0.64 us (1%)
    pallas_call x1, Pallas kernels, on_device(): pl.pallas_call(round_kernel, name='power_round', out_shape=(jax.ShapeDtyp...  52.8 us
    pallas_call x1, Pallas kernels, on_device(): pl.pallas_call(output_kernel, name='outputs', out_shape=(jax.ShapeDtypeSt...  2.46 us

profile of v11, /device:TPU:1, one launch (start us, length us, event | category | flops | bytes accessed | tf_op | source)
XLA Modules:
  0.0 55.9 jit_solution(18219720321844823282)
XLA Ops:
  0.6 52.8 %power_round.1 = (f32[240,1792]{1,0:T(8,128)S(1)}, bf16[128,1792]{1,0:T(8,128)(2,1)S(1)}, f32[240,64]{1,0:T(8,128)S(1)}, f32[1,64,240]{2,1,0:T(8,128)S(1)}) custom-call(bf16[1,240,1792]{2,1,0:T(8,128)(2,1)} %g_hbm.1, f32[1,240,1792]{2,1,0:T(8,128)} %e_hbm.1, f32[1,64,240]{2,1,0:T(8,128)} %bitcast.2), custom_call_target="tpu_custom_call" | custom-call | tf_op jit(solution)/shard_map/power_round/pallas_call | solution.py:317
  53.4 2.5 %outputs.1 = (bf16[240,1792]{1,0:T(8,128)(2,1)}, f32[1,240,1792]{2,1,0:T(8,128)}, f32[1,64,240]{2,1,0:T(8,128)}) custom-call(f32[240,1792]{1,0:T(8,128)S(1)} %get-tuple-element.10.m_ref, bf16[128,1792]{1,0:T(8,128)(2,1)S(1)} %get-tuple-element.11.p_ref, f32[240,64]{1,0:T(8,128)S(1)} %get-tuple-element.12.v_ref, f32[1,64,240]{2,1,0:T(8,128)S(1)} %get-tuple-element.13.q_ref), custom_call_target="tpu_custom_call" | custom-call | tf_op jit(solution)/shard_map/outputs/pallas_call | solution.py:361
